TPU v7x, 32 devices: a whole 2x2x4 slice. The times are simulated.
32 devices in a mesh: wide: 8 (over z, x), narrow: 4 (over y, core).
Axes of the slice: x: 2, y: 2, z: 4, core: 2. Of those that a mesh axis runs over, the one named last changes fastest.
Arguments:
- positions: float32 [3, 1572864], P(None, ('wide', 'narrow')), may hold values from -6 to 6
- velocities: float32 [3, 1572864], P(None, ('wide', 'narrow')), may hold values from -6 to 6
- nodal_mass: float32 [1572864], P(('wide', 'narrow')), may hold values from 0.5 to 2
- thickness: float32 [1572864], P(('wide', 'narrow')), may hold values from 0.05 to 0.3
- pack_index: int32 [32, 65536], P(('wide', 'narrow')), may hold values from 0 to 49152, as said below
- connectivity: int32 [65536, 4], P(('wide', 'narrow')), may hold values from 0 to 65535, as said below
- tile_list: int32 [2, 32768], P(None, ('wide', 'narrow')), may hold values from 0 to 511, as said below
- pair_mask: int32 [32768, 256], P(('wide', 'narrow')), may hold values 0 or 1
- tile_count: int32 [32], P(('wide', 'narrow')), may hold values from 256 to 1024
Outputs:
- contact_force: float32 [3, 1572864], P(None, ('wide', 'narrow'))
Inputs may be any that keep to these rules, and one draw needn't show every extreme that they name: `pack_index`: row s lists, for each send slot p * 2048 + k of mesh owner s (bound for partition p), the local node it carries, or 49152 for an empty slot. Each of the 49152 local nodes appears exactly once in its row; every block of 2048 slots carries at least 512 nodes, and in every row one block is full. `connectivity`: rows p * 2048 to (p + 1) * 2048 - 1 are partition p's segments; each entry is a non-empty slot of contact_state[p], and the 8192 entries of one partition are distinct. `tile_list`: row 0 holds node blocks below 512, row 1 segment blocks below 24. Within one partition's 1024 entries the first 512 node blocks are distinct and entry t + 512 has the node block of entry t.
All inputs are finite; a program needn't handle non-finite values. No bound on the sum of `pair_mask` on one device may be relied on, other than what follows from the above.
Results may differ from a plain program's by a relative error of at most 0.0003.
Values sent between devices are 32-bit elements; how exact they have to be, the bound alone decides.
No kernel may reach another device: no remote copies, remote signals or barrier semaphores. Data moves between devices by JAX's collectives and lax.ppermute only.
A program may use at most 128 MiB of HBM per device.

v0:
```python
import jax
import jax.numpy as jnp
from jax import lax
from jax.sharding import PartitionSpec as P

stiffness = 1.0
damping = 0.3
tiles_per_turn = 32


def padded(cells, sides, width):
    for axis, dim in sides:
        count = lax.axis_size(axis)
        ends = count - 1
        head = lax.slice_in_dim(cells, 0, width, axis=dim)
        tail = lax.slice_in_dim(cells, cells.shape[dim] - width, cells.shape[dim], axis=dim)
        cells = jnp.concatenate(
            [
                lax.ppermute(tail, axis, [(i, (i + 1) % count) for i in range(ends)]),
                cells,
                lax.ppermute(head, axis, [((i + 1) % count, i) for i in range(ends)]),
            ],
            axis=dim,
        )
    return cells


def quad_features(quad_nodes):
    corner = quad_nodes[:, 0:3]
    motion = quad_nodes[:, 3:6]
    centre = (corner[0] + corner[1] + corner[2] + corner[3]) * 0.25
    diag_one = corner[2] - corner[0]
    diag_two = corner[3] - corner[1]
    cross_raw = jnp.stack(
        [
            diag_one[1] * diag_two[2] - diag_one[2] * diag_two[1],
            diag_one[2] * diag_two[0] - diag_one[0] * diag_two[2],
            diag_one[0] * diag_two[1] - diag_one[1] * diag_two[0],
        ]
    )
    length = jnp.sqrt(jnp.sum(cross_raw * cross_raw, axis=0))
    normal = cross_raw / jnp.maximum(length, 1.0)
    drift = (motion[0] + motion[1] + motion[2] + motion[3]) * 0.25
    spread = jnp.sum((corner - centre[None]) ** 2, axis=(0, 1)) * 0.25
    return jnp.concatenate([centre, normal, drift, spread[None]], axis=0)


def neighbour_cells(ghost_rim):
    flat = ghost_rim.reshape((9,) + ghost_rim.shape[2:])
    return jnp.take(flat, jnp.array([0, 1, 2, 3, 5, 6, 7, 8], dtype=jnp.int32), axis=0)


def pair_forces(node_tile, seg_tile, mask_tile):
    position = node_tile[:, 0:3, :, None]
    centre = seg_tile[:, 0:3, None, :]
    normal = seg_tile[:, 3:6, None, :]
    signed_gap = (
        jnp.sum(position * normal, axis=1)
        - jnp.sum(centre * normal, axis=1)
        - node_tile[:, 7, :, None]
    )
    intersection = jnp.maximum(-signed_gap, 0.0)
    distance = jnp.sum((position - centre) ** 2, axis=1)
    weight = jnp.exp(-distance / (seg_tile[:, 9, None, :] + 0.25)) * mask_tile[:, None, :]
    closing = jnp.sum((node_tile[:, 3:6, :, None] - seg_tile[:, 6:9, None, :]) * normal, axis=1)
    magnitude = intersection * weight * (stiffness * node_tile[:, 6, :, None] - damping * closing)
    return jnp.sum(magnitude[:, None] * normal, axis=3)


def contact_pass(arrived, seg_all, tile_rows, mask_rows, tile_total):
    block_count = arrived.shape[1] // 128
    node_blocks = jnp.transpose(arrived.reshape(arrived.shape[0], block_count, 128), (1, 0, 2))
    seg_blocks = jnp.transpose(
        seg_all.reshape(seg_all.shape[0], seg_all.shape[1] // 256, 256), (1, 0, 2)
    )
    turns = (tile_total + tiles_per_turn - 1) // tiles_per_turn

    def one_turn(turn_index, totals):
        first_tile = (turn_index * tiles_per_turn).astype(jnp.int32)
        chosen = lax.dynamic_slice_in_dim(tile_rows, first_tile, tiles_per_turn, 1)
        mask_tile = lax.dynamic_slice_in_dim(mask_rows, first_tile, tiles_per_turn, 0).astype(
            jnp.float32
        )
        node_tile = jnp.take(node_blocks, chosen[0], axis=0)
        seg_tile = jnp.take(seg_blocks, chosen[1], axis=0)
        live_tiles = (first_tile + jnp.arange(tiles_per_turn, dtype=jnp.int32) < tile_total).astype(
            jnp.float32
        )
        tile_force = pair_forces(node_tile, seg_tile, mask_tile) * live_tiles[:, None, None]
        return totals.at[chosen[0]].add(tile_force)

    totals = lax.fori_loop(0, turns, one_turn, jnp.zeros((block_count, 3, 128), jnp.float32))
    return jnp.transpose(totals, (1, 0, 2)).reshape(3, -1)


def on_device(
    positions,
    velocities,
    nodal_mass,
    thickness,
    pack_index,
    connectivity,
    tile_list,
    pair_mask,
    tile_count,
):
    node_data = jnp.concatenate([positions, velocities, nodal_mass[None], thickness[None]], axis=0)
    slots_row = pack_index[0]
    outgoing = jnp.take(node_data, slots_row, axis=1, mode="fill", fill_value=0.0)
    arrived = lax.all_to_all(outgoing, ("wide", "narrow"), split_axis=1, concat_axis=1, tiled=True)
    quad_nodes = jnp.transpose(jnp.take(arrived[0:6], connectivity, axis=1), (2, 0, 1))
    ghost_count = connectivity.shape[0] // 4
    features = quad_features(quad_nodes)
    raw_quads = quad_nodes[:, :, :ghost_count].reshape(24, ghost_count)
    ghost_rim = padded(raw_quads[None, None], (("wide", 0), ("narrow", 1)), 1)
    cells = neighbour_cells(ghost_rim).reshape(8, 4, 6, ghost_count)
    ghost = quad_features(jnp.transpose(cells, (1, 2, 0, 3)).reshape(4, 6, 8 * ghost_count))
    seg_all = jnp.concatenate([features, ghost], axis=1)
    slot_force = contact_pass(arrived, seg_all, tile_list, pair_mask, tile_count[0])
    returned = lax.all_to_all(
        slot_force, ("wide", "narrow"), split_axis=1, concat_axis=1, tiled=True
    )
    slot_numbers = jnp.arange(slots_row.shape[0], dtype=jnp.int32)
    slot_of_node = (
        jnp.zeros((positions.shape[1],), jnp.int32).at[slots_row].set(slot_numbers, mode="drop")
    )
    return jnp.take(returned, slot_of_node, axis=1)


def solution(mesh):
    return jax.shard_map(
        on_device,
        mesh=mesh,
        in_specs=(
            P(None, ("wide", "narrow")),
            P(None, ("wide", "narrow")),
            P(("wide", "narrow")),
            P(("wide", "narrow")),
            P(("wide", "narrow"), None),
            P(("wide", "narrow"), None),
            P(None, ("wide", "narrow")),
            P(("wide", "narrow"), None),
            P(("wide", "narrow")),
        ),
        out_specs=P(None, ("wide", "narrow")),
        check_vma=False,
    )
```

profile of v0, /device:TPU:0, one launch (start us, length us, event | category | flops | bytes accessed | tf_op | source)
XLA Modules:
  0.0 1456.9 jit_solution(12697315389057678184)
XLA Ops:
  3.6 12.9 copy.77
  16.5 223.7 %gather_fusion.2 = f32[65536,8]{1,0:T(8,128)} fusion(f32[8,49152]{0,1:T(8,128)} %copy.77, s32[65536]{0:T(1024)S(1)} %broadcast_clamp_fusion), kind=kCustom, calls=%fused_computation.2 | custom fusion | bytes 4456448 | tf_op jit(solution)/shard_map/jit(_take)/gather | solution.py:109
  240.2 17.4 %copy.78 = f32[8,32,2048]{2,0,1:T(8,128)S(1)} copy(f32[8,32,2048]{0,2,1:T(8,128)} %bitcast.138) | data formatting | bytes 4194304 | tf_op jit(solution)/shard_map/jit(_take)/gather | solution.py:109
  261.2 7.3 all-to-all-start
  270.2 239.7 %scatter_custom_fusion.1 = s32[49152]{0:T(1024)S(1)} fusion(s32[65536]{0:T(1024)S(1)} %bitcast.149, s32[65536]{0:T(1024)S(1)} %iota.8, s32[]{:T(128)} %constant.101.clone.1), kind=kCustom, calls=%fused_computation.52 | custom fusion | bytes 196612 | tf_op jit(solution)/shard_map/scatter | solution.py:125
  510.0 15.5 %copy.80 = f32[6,32,2048]{0,2,1:T(8,128)} copy(f32[6,32,2048]{2,0,1:T(8,128)S(1)} %bitcast.140) | data formatting | bytes 3145728 | tf_op jit(solution)/shard_map/slice | solution.py:111
  525.5 38.2 %gather_fusion.3 = f32[8192,6]{1,0:T(8,128)} fusion(f32[6,65536]{0,1:T(8,128)} %bitcast.136, s32[8192]{0:T(1024)S(1)} %broadcast_clamp_fusion.1), kind=kCustom, calls=%fused_computation.3 | custom fusion | bytes 425984 | tf_op jit(solution)/shard_map/jit(_take)/gather | solution.py:111
  567.4 3.7 collective-permute-start
  589.4 282.9 %while.10 = (s32[]{:T(128)}, f32[512,3,128]{2,1,0:T(4,128)}, s32[]{:T(128)}, s32[2,1024]{1,0:T(2,128)}, f32[512,8,128]{2,1,0:T(8,128)}, /*index=5*/f32[24,10,256...) while((s32[]{:T(128)}, f32[512,3,128]{2,1,0:T(4,128)}, ...), condition=%wide.region_12.13_spmd, body=%wide.region_5.0_spmd.sunk | while | flops 40032932 | bytes 37398960 | solution.py:92
  593.4 5.4 multiply_reduce_fusion.11
  612.2 5.4 multiply_reduce_fusion.11
  631.0 5.4 multiply_reduce_fusion.11
  649.9 5.4 multiply_reduce_fusion.11
  668.8 5.4 multiply_reduce_fusion.11
  687.7 5.4 multiply_reduce_fusion.11
  706.5 5.4 multiply_reduce_fusion.11
  725.3 5.4 multiply_reduce_fusion.11
  744.2 5.4 multiply_reduce_fusion.11
  763.1 5.4 multiply_reduce_fusion.11
  781.9 5.4 multiply_reduce_fusion.11
  800.7 5.4 multiply_reduce_fusion.11
  812.0 3.7 scatter_fusion
  819.6 5.4 multiply_reduce_fusion.11
  838.5 5.4 multiply_reduce_fusion.11
  857.3 5.4 multiply_reduce_fusion.11
  868.6 3.7 scatter_fusion
  872.3 328.9 %all-to-all-start.1 = ((f32[3,32,2048]{2,0,1:T(4,128)}), f32[3,32,2048]{2,0,1:T(4,128)S(1)}, u32[]{:S(2)}, u32[]{:S(2)}) async-start(f32[3,32,2048]{2,0,1:T(4,128)} %bitcast.38), calls=%async_computation.1 | async-start | bytes 2097152 | tf_op jit(solution)/shard_map/all_to_all | solution.py:120
  1201.3 26.1 %all-to-all-done.1 = f32[3,32,2048]{2,0,1:T(4,128)S(1)} async-done(((f32[3,32,2048]{2,0,1:T(4,128)}), f32[3,32,2048]{2,0,1:T(4,128)S(1)}, u32[]{:S(2)}, u32[]{:S(2)}) %all-to-all-start.1) | async-done | bytes 786464 | tf_op jit(solution)/shard_map/all_to_all | solution.py:120
  1227.5 15.4 %copy.94 = f32[3,32,2048]{0,2,1:T(8,128)} copy(f32[3,32,2048]{2,0,1:T(4,128)S(1)} %all-to-all-done.1) | data formatting | bytes 1572864 | tf_op jit(solution)/shard_map/all_to_all | solution.py:120
  1242.9 172.4 %gather_fusion.5 = f32[49152,3]{1,0:T(8,128)} fusion(f32[3,65536]{0,1:T(8,128)} %bitcast.137, s32[49152]{0:T(1024)S(1)} %fusion.4), kind=kCustom, calls=%fused_computation.5 | custom fusion | bytes 1376256 | tf_op jit(solution)/shard_map/jit(_take)/gather | solution.py:127
  1415.3 27.4 %select_bitcast_fusion = f32[3,49152]{0,1:T(8,128)} fusion(f32[49152,3]{1,0:T(8,128)} %gather_fusion.5, pred[49152]{0:T(1024)(128)(4,1)S(1)} %compare_and_fusion.3), kind=kLoop, calls=%fused_computation.32 | loop fusion | flops 147456 | bytes 1228800 | tf_op jit(solution)/shard_map/jit(_take)/select_n | solution.py:127
  1442.7 14.1 copy.95
  (351 shorter events, 222.8 us)
Async XLA Ops:
  240.2 18.0 %copy-start = (s32[1,65536]{1,0:T(1,128)S(1)}, s32[1,65536]{1,0:T(1,128)}, u32[]{:S(2)}) copy-start(s32[1,65536]{1,0:T(1,128)} %param.16) | copy-start | bytes 786436
  259.5 9.6 copy-start.1
  261.2 248.7 %copy-start.2 = (s32[8]{0:T(128)S(1)}, s32[8]{0:T(128)}, u32[]{:S(2)}) copy-start(s32[8]{0:T(128)} %constant.148) | copy-start | bytes 100
  261.2 248.8 %all-to-all-start = ((f32[8,32,2048]{2,0,1:T(8,128)}), f32[8,32,2048]{2,0,1:T(8,128)S(1)}, u32[]{:S(2)}, u32[]{:S(2)}) async-start(f32[8,32,2048]{2,0,1:T(8,128)} %broadcast_select_fusion.2), calls=%async_computation | async-start | bytes 4194304 | tf_op jit(solution)/shard_map/all_to_all | solution.py:110
  567.4 12.1 collective-permute-start
  571.1 8.5 collective-permute-start.1
  579.6 3.3 collective-permute-start.2
  581.4 4.5 collective-permute-start.3
  872.3 355.1 %all-to-all-start.1 = ((f32[3,32,2048]{2,0,1:T(4,128)}), f32[3,32,2048]{2,0,1:T(4,128)S(1)}, u32[]{:S(2)}, u32[]{:S(2)}) async-start(f32[3,32,2048]{2,0,1:T(4,128)} %bitcast.38), calls=%async_computation.1 | async-start | bytes 2097152 | tf_op jit(solution)/shard_map/all_to_all | solution.py:120
where the time goes:
time: 1460 us
  local copies, waits for them, and re-layouts  817 us (56%)
  starting transfers between devices  344 us (24%)
  other arithmetic  263 us (18%)
  waiting for transfers between devices  29.1 us (2%)
    all_to_all x1, starting transfers between devices, on_device(): lax.all_to_all(slot_force, ('wide', 'narrow'), split_axis=1, concat_axis=...  329 us
    gather x2, local copies, waits for them, and re-layouts, on_device(): jnp.take(node_data, slots_row, axis=1, mode='fill', fill_value=0.0)  241 us
    scatter x1, local copies, waits for them, and re-layouts, on_device(): jnp.zeros((positions.shape[1],), jnp.int32).at[slots_row]  240 us
    gather x1, local copies, waits for them, and re-layouts, on_device(): return jnp.take(returned, slot_of_node, axis=1)  172 us
    reduce_sum x15, other arithmetic, pair_forces(): jnp.sum(position * normal, axis=1) - jnp.sum(centre * normal, axis=1)  81 us
    scatter-add x15, other arithmetic, one_turn(): return totals.at[chosen[0]].add(tile_force)  54.6 us
    gather x2, local copies, waits for them, and re-layouts, on_device(): jnp.take(arrived[0:6], connectivity, axis=1)  41.8 us
    mul x15, other arithmetic, pair_forces(): intersection * weight  35.9 us
  transfers between devices with their start and end apart: 6, of which 2 were waited for; matrix products, arithmetic and copies ran while one was open for 17% of the time, Pallas kernels for 0%

commit v1 on v0

v1 whole, which is shorter than its diff:
```python
import math

import jax
import jax.numpy as jnp
from jax import lax
from jax.experimental import pallas as pl
from jax.experimental.pallas import tpu as pltpu
from jax.sharding import PartitionSpec as P

stiffness = 1.0
damping = 0.3
lanes = 128
groups = 16
span = lanes * groups
half_span = span // 2
seg_width = 256
table_unroll = 8
tiles_per_turn = 4
vmem_limit = 60 * 2**20
F32 = jnp.float32
BF16 = jnp.bfloat16
in_vmem = pl.BlockSpec(memory_space=pltpu.VMEM)
in_smem = pl.BlockSpec(memory_space=pltpu.SMEM)
in_hbm = pl.BlockSpec(memory_space=pl.ANY)


def fetch(index_ref, buffers, sems, turn, part):
    start = pl.multiple_of(turn * span + part * half_span, half_span)
    return pltpu.make_async_copy(
        index_ref.at[pl.ds(start, half_span)], buffers[part], sems.at[part]
    )


def each_slot(index_ref, buffers, sems, turns, before, move, after):
    for part in range(2):
        fetch(index_ref, buffers, sems, 0, part).start()

    def body(turn, carry):
        before(turn)
        for part in range(2):
            fetch(index_ref, buffers, sems, turn, part).wait()
            for j in range(lanes):
                for g in range(groups // 2):
                    move(buffers[part][g * lanes + j], j, part * (groups // 2) + g)

            @pl.when(turn + 1 < turns)
            def _():
                fetch(index_ref, buffers, sems, turn + 1, part).start()

        after(turn)
        return carry

    lax.fori_loop(0, turns, body, 0)


def pack_kernel(index_ref, nodes, out, table, rows, buffer_a, buffer_b, sems):
    count = nodes.shape[1]

    def fill(step, carry):
        for i in range(table_unroll):
            start = pl.multiple_of((step * table_unroll + i) * lanes, lanes)
            column = nodes[:, pl.ds(start, lanes)]
            table[pl.ds(start, lanes), :] = jnp.concatenate([column] * groups, axis=0).T
        return carry

    lax.fori_loop(0, count // (lanes * table_unroll), fill, 0)
    table[count : count + 8, :] = jnp.zeros((8, lanes), F32)

    def move(row, j, g):
        rows[j : j + 1, g * 8 : g * 8 + 8] = table[pl.ds(row, 1), g * 8 : g * 8 + 8]

    def after(turn):
        out[pl.ds(turn * groups, groups)] = rows[...].T.reshape(groups, 8, lanes)

    each_slot(
        index_ref,
        (buffer_a, buffer_b),
        sems,
        index_ref.shape[0] // span,
        lambda turn: None,
        move,
        after,
    )


def pack(slots_row, node_data):
    return pl.pallas_call(
        pack_kernel,
        out_shape=jax.ShapeDtypeStruct((slots_row.shape[0] // lanes, 8, lanes), F32),
        in_specs=[in_hbm, in_vmem],
        out_specs=in_vmem,
        scratch_shapes=[
            pltpu.VMEM((node_data.shape[1] + 8, lanes), F32),
            pltpu.VMEM((lanes, lanes), F32),
            pltpu.SMEM((half_span,), jnp.int32),
            pltpu.SMEM((half_span,), jnp.int32),
            pltpu.SemaphoreType.DMA((2,)),
        ],
        compiler_params=pltpu.CompilerParams(vmem_limit_bytes=vmem_limit),
    )(slots_row, node_data)


def unpack_kernel(index_ref, forces, out, table, stage, rows, buffer_a, buffer_b, sems):
    count = out.shape[1]

    def clear(step, carry):
        start = pl.multiple_of(step * lanes, lanes)
        table[pl.ds(start, lanes), :] = jnp.zeros((lanes, lanes), F32)
        return carry

    lax.fori_loop(0, count // lanes, clear, 0)
    stage[...] = jnp.zeros(stage.shape, F32)

    def before(turn):
        for f in range(3):
            stage[pl.ds(f, groups, stride=8), :] = forces[f, pl.ds(turn * groups, groups), :]
        rows[...] = stage[...].T

    def move(row, j, g):
        table[pl.ds(row, 1), g * 8 : g * 8 + 8] = rows[j : j + 1, g * 8 : g * 8 + 8]

    each_slot(
        index_ref,
        (buffer_a, buffer_b),
        sems,
        index_ref.shape[0] // span,
        before,
        move,
        lambda turn: None,
    )

    def drain(step, carry):
        for i in range(table_unroll):
            start = pl.multiple_of((step * table_unroll + i) * lanes, lanes)
            turned = table[pl.ds(start, lanes), :].T.reshape(groups, 8, lanes)
            out[:, pl.ds(start, lanes)] = jnp.sum(turned, axis=0)[0:3]
        return carry

    lax.fori_loop(0, count // (lanes * table_unroll), drain, 0)


def unpack(slots_row, forces, count):
    return pl.pallas_call(
        unpack_kernel,
        out_shape=jax.ShapeDtypeStruct((3, count), F32),
        in_specs=[in_hbm, in_vmem],
        out_specs=in_vmem,
        scratch_shapes=[
            pltpu.VMEM((count + 8, lanes), F32),
            pltpu.VMEM((lanes, lanes), F32),
            pltpu.VMEM((lanes, lanes), F32),
            pltpu.SMEM((half_span,), jnp.int32),
            pltpu.SMEM((half_span,), jnp.int32),
            pltpu.SemaphoreType.DMA((2,)),
        ],
        compiler_params=pltpu.CompilerParams(vmem_limit_bytes=vmem_limit),
    )(slots_row, forces)


def quad_features(corners):
    x = [c[0:3] for c in corners]
    v = [c[3:6] for c in corners]
    centre = (x[0] + x[1] + x[2] + x[3]) * 0.25
    a = x[2] - x[0]
    b = x[3] - x[1]
    cross = jnp.concatenate(
        [
            a[1:2] * b[2:3] - a[2:3] * b[1:2],
            a[2:3] * b[0:1] - a[0:1] * b[2:3],
            a[0:1] * b[1:2] - a[1:2] * b[0:1],
        ],
        axis=0,
    )
    length = jnp.sqrt(jnp.sum(cross * cross, axis=0, keepdims=True))
    normal = cross / jnp.maximum(length, 1.0)
    drift = (v[0] + v[1] + v[2] + v[3]) * 0.25
    apart = sum((xi - centre) ** 2 for xi in x)
    spread = jnp.sum(apart, axis=0, keepdims=True) * 0.25
    return jnp.concatenate(
        [centre, normal, drift, spread, jnp.zeros((6, lanes), F32)], axis=0
    )


def feature_kernel(corner_ref, nodes, out):
    quads = corner_ref.shape[1]
    lane = lax.broadcasted_iota(jnp.int32, (8, lanes), 1)

    def one_block(block, half):
        corners = []
        for i in range(4):
            state = jnp.zeros((8, lanes), F32)
            for j in range(lanes):
                slot = corner_ref[i, block * lanes + j]
                moved = pltpu.roll(nodes[slot >> 7], (j - slot) & 127, axis=1)
                state = jnp.where(lane == j, moved, state)
            corners.append(state)
        out[block // 2, :, half * lanes : (half + 1) * lanes] = quad_features(corners)

    def body(pair, carry):
        one_block(pair * 2, 0)
        one_block(pair * 2 + 1, 1)
        return carry

    lax.fori_loop(0, quads // seg_width, body, 0)


def segment_features(corner_slots, node_blocks):
    return pl.pallas_call(
        feature_kernel,
        out_shape=jax.ShapeDtypeStruct((corner_slots.shape[1] // seg_width, 16, seg_width), F32),
        in_specs=[in_smem, in_vmem],
        out_specs=in_vmem,
        compiler_params=pltpu.CompilerParams(vmem_limit_bytes=vmem_limit),
    )(corner_slots, node_blocks)


def three_parts(x):
    first = x.astype(BF16).astype(F32)
    rest = x - first
    second = rest.astype(BF16).astype(F32)
    return first, second, rest - second


def segment_rows(f):
    centre, normal, drift, spread = f[0:3], f[3:6], f[6:9], f[9:10]
    zero = jnp.zeros_like(spread)
    one = jnp.ones_like(spread)
    zeros = jnp.zeros_like(centre)
    rate = math.log2(math.e) / (spread + 0.25)
    plane = jnp.sum(centre * normal, axis=0, keepdims=True)
    square = jnp.sum(centre * centre, axis=0, keepdims=True)
    slide = jnp.sum(drift * normal, axis=0, keepdims=True)
    depth = [-normal, zeros, zero, one, zero, plane, zeros, zeros]
    power = [(2.0 * rate) * centre, zeros, zero, zero, -rate, -(rate * square), zeros, zeros]
    push = [zeros, -damping * normal, stiffness * one, zero, zero, damping * slide, zeros, zeros]
    return [jnp.concatenate(rows, axis=0) for rows in (depth, power, push)]


def contact_kernel(count_ref, list_ref, nodes, features, mask, out, seg_side, normals):
    def prepare(block, carry):
        f = features[block]
        for i, rows in enumerate(segment_rows(f)):
            p, q, r = three_parts(rows)
            seg_side[block, :, i * seg_width : (i + 1) * seg_width] = jnp.concatenate(
                [p, q, r, p, q, p], axis=0
            ).astype(BF16)
        padded = jnp.concatenate([f[3:6], jnp.zeros((5, seg_width), F32)], axis=0)
        p, q, r = three_parts(padded)
        normals[block] = jnp.concatenate([p, q], axis=0)
        return carry

    lax.fori_loop(0, features.shape[0], prepare, 0)
    out[...] = jnp.zeros(out.shape, F32)
    count = count_ref[0]
    per_owner = out.shape[2]
    row = lax.broadcasted_iota(jnp.int32, (8, lanes), 0)
    by_last = (((1,), (1,)), ((), ()))
    by_first = (((0,), (0,)), ((), ()))

    def tile_force(t):
        state = nodes[list_ref[0, t]]
        block = list_ref[1, t]
        square = jnp.sum(jnp.where(row < 3, state * state, 0.0), axis=0, keepdims=True)
        extra = jnp.where(row == 0, square, jnp.where(row == 1, 1.0, 0.0))
        p, q, r = three_parts(jnp.concatenate([state, extra], axis=0))
        node_side = jnp.concatenate([p, p, p, q, q, r], axis=0).astype(BF16)
        pairs = lax.dot_general(node_side, seg_side[block], by_first, preferred_element_type=F32)
        magnitude = (
            jnp.maximum(pairs[:, 0:seg_width], 0.0)
            * jnp.exp2(pairs[:, seg_width : 2 * seg_width])
            * pairs[:, 2 * seg_width :]
        )
        high = magnitude.astype(BF16)
        low = (magnitude - high.astype(F32)).astype(BF16)
        live = jnp.where(t < count, 1.0, 0.0)
        chosen = (normals[block] * (mask[pl.ds(t, 1), :].astype(F32) * live)).astype(BF16)
        force = lax.dot_general(
            chosen, high, by_last, preferred_element_type=F32
        ) + lax.dot_general(chosen, low, by_last, preferred_element_type=F32)
        return force[0:8] + force[8:16]

    half = list_ref.shape[1] // 2

    def phase(start, total, add):
        def turn(index, carry):
            first = start + index * tiles_per_turn
            made = [tile_force(first + k) for k in range(tiles_per_turn)]
            for k, force in enumerate(made):
                block = list_ref[0, first + k]
                owner = block // per_owner
                at = pl.ds(block % per_owner, 1)
                for f in range(3):
                    if add:
                        out[owner, f, at, :] += force[f : f + 1]
                    else:
                        out[owner, f, at, :] = force[f : f + 1]
            return carry

        lax.fori_loop(0, (total + tiles_per_turn - 1) // tiles_per_turn, turn, 0)

    phase(0, jnp.minimum(count, half), False)
    phase(half, jnp.maximum(count - half, 0), True)


def contact_pass(tile_count, tile_list, node_blocks, features, pair_mask, owners):
    blocks = node_blocks.shape[0]
    return pl.pallas_call(
        contact_kernel,
        out_shape=jax.ShapeDtypeStruct((owners, 3, blocks // owners, lanes), F32),
        in_specs=[in_smem, in_smem, in_vmem, in_vmem, in_vmem],
        out_specs=in_vmem,
        scratch_shapes=[
            pltpu.VMEM((features.shape[0], 96, 3 * seg_width), BF16),
            pltpu.VMEM((features.shape[0], 16, seg_width), F32),
        ],
        compiler_params=pltpu.CompilerParams(vmem_limit_bytes=vmem_limit),
    )(tile_count, tile_list, node_blocks, features, pair_mask)


def with_neighbours(cells, axis):
    count = lax.axis_size(axis)
    up = [(i, i + 1) for i in range(count - 1)]
    down = [(i + 1, i) for i in range(count - 1)]
    return jnp.stack([lax.ppermute(cells, axis, up), cells, lax.ppermute(cells, axis, down)])


def on_device(
    positions,
    velocities,
    nodal_mass,
    thickness,
    pack_index,
    connectivity,
    tile_list,
    pair_mask,
    tile_count,
):
    both = ("wide", "narrow")
    owners = lax.axis_size("wide") * lax.axis_size("narrow")
    node_data = jnp.concatenate([positions, velocities, nodal_mass[None], thickness[None]], axis=0)
    slots_row = pack_index.reshape(-1)
    outgoing = pack(slots_row, node_data)
    per_owner = outgoing.shape[0] // owners
    arrived = lax.all_to_all(
        outgoing.reshape(owners, per_owner, 8, lanes), both, split_axis=0, concat_axis=0
    ).reshape(-1, 8, lanes)
    own = segment_features(connectivity.T, arrived)
    edge = connectivity.shape[0] // 4 // seg_width
    rim = with_neighbours(with_neighbours(own[:edge], "wide"), "narrow")
    ghosts = [rim[db, da] for da in range(3) for db in range(3) if (da, db) != (1, 1)]
    features = jnp.concatenate([own] + ghosts, axis=0)
    slot_force = contact_pass(tile_count, tile_list, arrived, features, pair_mask, owners)
    returned = lax.all_to_all(slot_force, both, split_axis=0, concat_axis=0)
    forces = jnp.transpose(returned, (1, 0, 2, 3)).reshape(3, -1, lanes)
    return unpack(slots_row, forces, positions.shape[1])


def solution(mesh):
    return jax.shard_map(
        on_device,
        mesh=mesh,
        in_specs=(
            P(None, ("wide", "narrow")),
            P(None, ("wide", "narrow")),
            P(("wide", "narrow")),
            P(("wide", "narrow")),
            P(("wide", "narrow"), None),
            P(("wide", "narrow"), None),
            P(None, ("wide", "narrow")),
            P(("wide", "narrow"), None),
            P(("wide", "narrow")),
        ),
        out_specs=P(None, ("wide", "narrow")),
        check_vma=False,
    )
```

time: 1460 us -> 502 us (0.34)
  local copies, waits for them, and re-layouts: 817 us -> 3.42 us
  starting transfers between devices: 344 us -> 7.24 us
  blocking collectives: 0 us -> 263 us
  other arithmetic: 263 us -> 3.45 us
  Pallas kernels: 0 us -> 214 us
  waiting for transfers between devices: 29.1 us -> 7.44 us
    gather x37 -> x0, local copies, waits for them, and re-layouts: 497 us -> none  [the longest x2 241 us: on_device(): jnp.take(node_data, slots_row, axis=1, mode='fill', fill_value=0.0)]
    all_to_all x2 -> x0, starting transfers between devices: 336 us -> none  [the longest x1 329 us: on_device(): lax.all_to_all(slot_force, ('wide', 'narrow'), split_axis=1, concat_axis=...]
    all_to_all x0 -> x2, blocking collectives: none -> 263 us  [the longest x1 207 us: on_device(): returned = lax.all_to_all(slot_force, both, split_axis=0, concat_axis=0)]
    scatter x1 -> x0, local copies, waits for them, and re-layouts: 240 us -> none  [on_device(): jnp.zeros((positions.shape[1],), jnp.int32).at[slots_row]]
    pallas_call x0 -> x4, Pallas kernels: none -> 214 us  [the longest x1 78.3 us: contact_pass(): pl.pallas_call(contact_kernel, out_shape=jax.ShapeDtypeStruct((owners, 3,...]
    reduce_sum x49 -> x0, other arithmetic: 111 us -> none  [the longest x15 81 us: pair_forces(): jnp.sum(position * normal, axis=1) - jnp.sum(centre * normal, axis=1)]
    scatter-add x15 -> x0, other arithmetic: 54.6 us -> none  [one_turn(): return totals.at[chosen[0]].add(tile_force)]
    mul x36 -> x0, other arithmetic: 37.8 us -> none  [the longest x15 35.9 us: pair_forces(): intersection * weight]
  transfers between devices with their start and end apart: 6 -> 4, of which waited for: 2 -> 2; matrix products, arithmetic and copies ran while one was open for 17% -> 0% of each run, Pallas kernels for 0% -> 0%
where the time goes in v1:
time: 502 us; the launch traced here: 499 us
  blocking collectives  263 us (52%)
  Pallas kernels  214 us (43%)
  waiting for transfers between devices  7.44 us (1%)
  starting transfers between devices  7.24 us (1%)
    all_to_all x1, blocking collectives, on_device(): returned = lax.all_to_all(slot_force, both, split_axis=0, concat_axis=0)  207 us
    pallas_call x1, Pallas kernels, contact_pass(): pl.pallas_call(contact_kernel, out_shape=jax.ShapeDtypeStruct((owners, 3,...  78.3 us
    all_to_all x1, blocking collectives, on_device(): lax.all_to_all(outgoing.reshape(owners, per_owner, 8, lanes), both, split...  56.1 us
    pallas_call x1, Pallas kernels, unpack(): pl.pallas_call(unpack_kernel, out_shape=jax.ShapeDtypeStruct((3, count),...  54.9 us
    pallas_call x1, Pallas kernels, pack(): pl.pallas_call(pack_kernel, out_shape=jax.ShapeDtypeStruct((slots_row.sha...  54.2 us
    pallas_call x1, Pallas kernels, segment_features(): pl.pallas_call(feature_kernel, out_shape=jax.ShapeDtypeStruct((corner_slo...  26.3 us
  transfers between devices with their start and end apart: 4, of which 2 were waited for; matrix products, arithmetic and copies ran while one was open for 0% of the time, Pallas kernels for 0%

profile of v1, /device:TPU:0, one launch (start us, length us, event | category | flops | bytes accessed | tf_op | source)
XLA Modules:
  0.0 498.7 jit_solution(12410821812644990773)
XLA Ops:
  0.0 3.4 pad_maximum_fusion.nodes
  3.4 54.2 %shard_map.91 = f32[512,8,128]{2,1,0:T(8,128)} custom-call(s32[65536]{0:T(1024)} %bitcast.53, f32[8,49152]{1,0:T(8,128)} %pad_maximum_fusion.nodes), custom_call_target="tpu_custom_call" | custom-call | tf_op jit(solution)/shard_map/pallas_call | solution.py:87
  57.6 56.1 %all_to_all.10 = f32[32,16,8,128]{3,2,1,0:T(8,128)} all-to-all(f32[32,16,8,128]{3,2,1,0:T(8,128)} %bitcast.50), channel_id=1, replica_groups=mesh['wide'=8,'narrow'=4] {'wide','narrow'}, dimensions={0} | all-to-all | bytes 4194304 | tf_op jit(solution)/shard_map/all_to_all | solution.py:344
  113.8 26.3 %shard_map.92 = f32[8,16,256]{2,1,0:T(8,128)} custom-call(s32[4,2048]{1,0:T(4,128)} %bitcast.63, f32[512,8,128]{2,1,0:T(8,128)} %bitcast.48), custom_call_target="tpu_custom_call" | custom-call | tf_op jit(solution)/shard_map/pallas_call | solution.py:208
  140.1 0.8 slice_bitcast_fusion.8
  140.9 3.4 collective-permute-start
  144.2 1.3 collective-permute-start.1
  146.2 0.0 collective-permute-done
  146.2 3.9 collective-permute-done.1
  150.0 1.3 collective-permute-start.2
  151.4 0.9 constant_dynamic-update-slice_fusion
  152.3 1.3 collective-permute-start.3
  153.6 0.0 collective-permute-done.2
  153.6 3.6 collective-permute-done.3
  157.3 0.0 copy-start
  157.3 0.7 copy-done
  158.0 78.3 %shard_map.93 = f32[32,3,16,128]{3,2,1,0:T(8,128)} custom-call(s32[1]{0:T(128)S(6)} %copy.19.count_ref, s32[2,1024]{1,0:T(2,128)} %list_ref.1, f32[512,8,128]{2,1,0:T(8,128)} %bitcast.49, f32[24,16,256]{2,1,0:T(8,128)} %copy-done, s32[1024,256]{1,0:T(8,128)} %mask.1), custom_call_target="tpu_custom_call" | custom-call | tf_op jit(solution)/shard_map/pallas_call | solution.py:307
  236.3 206.5 %all_to_all.11 = f32[32,3,16,128]{3,2,1,0:T(8,128)S(1)} all-to-all(f32[32,3,16,128]{3,2,1,0:T(8,128)} %shard_map.93), channel_id=1, replica_groups=mesh['wide'=8,'narrow'=4] {'wide','narrow'}, dimensions={0} | all-to-all | bytes 1572864 | tf_op jit(solution)/shard_map/all_to_all | solution.py:353
  442.8 1.0 copy.10
  443.8 54.9 %shard_map.94 = f32[3,49152]{1,0:T(4,128)} custom-call(s32[65536]{0:T(1024)} %bitcast.54, f32[3,512,128]{2,1,0:T(8,128)} %bitcast.51), custom_call_target="tpu_custom_call" | custom-call | tf_op jit(solution)/shard_map/pallas_call | solution.py:143
  (9 shorter events, 0.1 us)
Async XLA Ops:
  140.9 5.3 %collective-permute-start = (f32[2,16,256]{2,1,0:T(8,128)S(1)}, f32[2,16,256]{2,1,0:T(8,128)S(1)}, u32[]{:S(2)}, u32[]{:S(2)}) collective-permute-start(f32[2,16,256]{2,1,0:T(8,128)S(1)} %get-tuple-element.6), channel_id=1, source_target_pairs={{0,4},{4,8},{8,12},{12,16},{16,20},{20,24},{24,28},{1,5},{5,9},{9,... | collective-permute-start | bytes 98312 | tf_op jit(solution)/shard_map/ppermute | solution.py:324
  144.2 5.8 %collective-permute-start.1 = (f32[2,16,256]{2,1,0:T(8,128)S(1)}, f32[2,16,256]{2,1,0:T(8,128)S(1)}, u32[]{:S(2)}, u32[]{:S(2)}) collective-permute-start(f32[2,16,256]{2,1,0:T(8,128)S(1)} %get-tuple-element.6), channel_id=1, source_target_pairs={{4,0},{8,4},{12,8},{16,12},{20,16},{24,20},{28,24},{5,1},{9,5},{13... | collective-permute-start | bytes 98312 | tf_op jit(solution)/shard_map/ppermute | solution.py:324
  150.0 3.5 collective-permute-start.2
  152.3 4.9 collective-permute-start.3
  157.3 0.8 copy-start

commit v2 on v1

--- a/solution.py
+++ b/solution.py
@@ -1,4 +1,5 @@
 import math
+from functools import partial
 
 import jax
 import jax.numpy as jnp
@@ -15,7 +16,8 @@
 half_span = span // 2
 seg_width = 256
 table_unroll = 8
-tiles_per_turn = 4
+pairs_per_turn = 8
+mask_power = 256.0
 vmem_limit = 60 * 2**20
 F32 = jnp.float32
 BF16 = jnp.bfloat16
@@ -181,17 +183,18 @@
     )
 
 
-def feature_kernel(corner_ref, nodes, out):
-    quads = corner_ref.shape[1]
+def feature_kernel(start_ref, nodes, place, out):
     lane = lax.broadcasted_iota(jnp.int32, (8, lanes), 1)
+    quad_blocks = place.shape[1]
 
     def one_block(block, half):
         corners = []
         for i in range(4):
+            where = jnp.broadcast_to(place[i, pl.ds(block, 1), :], (8, lanes))
             state = jnp.zeros((8, lanes), F32)
             for j in range(lanes):
-                slot = corner_ref[i, block * lanes + j]
-                moved = pltpu.roll(nodes[slot >> 7], (j - slot) & 127, axis=1)
+                start = pl.multiple_of(start_ref[i, block * lanes + j], 8)
+                moved = jnp.take_along_axis(nodes[pl.ds(start, 8), :], where, axis=1)
                 state = jnp.where(lane == j, moved, state)
             corners.append(state)
         out[block // 2, :, half * lanes : (half + 1) * lanes] = quad_features(corners)
@@ -201,17 +204,23 @@
         one_block(pair * 2 + 1, 1)
         return carry
 
-    lax.fori_loop(0, quads // seg_width, body, 0)
-
-
-def segment_features(corner_slots, node_blocks):
+    lax.fori_loop(0, quad_blocks // 2, body, 0)
+
+
+def segment_features(connectivity, node_blocks):
+    corner_slots = connectivity.T
+    quads = corner_slots.shape[1]
     return pl.pallas_call(
         feature_kernel,
-        out_shape=jax.ShapeDtypeStruct((corner_slots.shape[1] // seg_width, 16, seg_width), F32),
-        in_specs=[in_smem, in_vmem],
+        out_shape=jax.ShapeDtypeStruct((quads // seg_width, 16, seg_width), F32),
+        in_specs=[in_smem, in_vmem, in_vmem],
         out_specs=in_vmem,
         compiler_params=pltpu.CompilerParams(vmem_limit_bytes=vmem_limit),
-    )(corner_slots, node_blocks)
+    )(
+        corner_slots // lanes * 8,
+        node_blocks.reshape(-1, lanes),
+        (corner_slots % lanes).reshape(4, -1, lanes),
+    )
 
 
 def three_parts(x):
@@ -236,92 +245,214 @@
     return [jnp.concatenate(rows, axis=0) for rows in (depth, power, push)]
 
 
-def contact_kernel(count_ref, list_ref, nodes, features, mask, out, seg_side, normals):
+def pair_kernel(
+    own_blocks, count_ref, list_ref, total, first_own, second_own, first_far, second_far, waiting
+):
+    blocks = waiting.shape[0]
+    for block in range(blocks):
+        waiting[block] = -1
+
+    def match(t, counts):
+        own_count, far_count = counts
+        block = list_ref[1, t]
+        other = waiting[block]
+        met = (other >= 0).astype(jnp.int32)
+        first_own[own_count] = other
+        second_own[own_count] = t
+        first_far[far_count] = other
+        second_far[far_count] = t
+        waiting[block] = jnp.where(other >= 0, -1, t)
+        is_own = block < own_blocks
+        return own_count + jnp.where(is_own, met, 0), far_count + jnp.where(is_own, 0, met)
+
+    own_count, far_count = lax.fori_loop(0, count_ref[0], match, (jnp.int32(0), jnp.int32(0)))
+
+    def leave(first, second):
+        def step(block, count):
+            other = waiting[block]
+            first[count] = other
+            second[count] = -1
+            return count + (other >= 0).astype(jnp.int32)
+
+        return step
+
+    own_count = lax.fori_loop(0, own_blocks, leave(first_own, second_own), own_count)
+    far_count = lax.fori_loop(own_blocks, blocks, leave(first_far, second_far), far_count)
+    for k in range(pairs_per_turn):
+        first_own[own_count + k] = -1
+        second_own[own_count + k] = -1
+        first_far[far_count + k] = -1
+        second_far[far_count + k] = -1
+    total[0] = own_count
+    total[1] = far_count
+
+
+def tile_pairs(tile_count, tile_list, own_blocks, blocks):
+    room = tile_list.shape[1] // 2 + blocks + pairs_per_turn
+    room = (room + lanes - 1) // lanes * lanes
+    listed = jax.ShapeDtypeStruct((room,), jnp.int32)
+    return pl.pallas_call(
+        partial(pair_kernel, own_blocks),
+        out_shape=[jax.ShapeDtypeStruct((2,), jnp.int32)] + [listed] * 4,
+        in_specs=[in_smem, in_smem],
+        out_specs=[in_smem] * 5,
+        scratch_shapes=[pltpu.SMEM((blocks,), jnp.int32)],
+    )(tile_count, tile_list)
+
+
+def contact_kernel(
+    first_block, total_ref, firsts, seconds, list_ref, source_ref, live_ref,
+    nodes, features, mask, before, out, seg_side, normals, masked,
+):
+    rows128 = lax.broadcasted_iota(jnp.int32, (lanes, lanes), 0)
+    chunk = 16
+    chunks = seg_width // chunk
+
     def prepare(block, carry):
-        f = features[block]
-        for i, rows in enumerate(segment_rows(f)):
+        f = features[source_ref[block]] * live_ref[block].astype(F32)
+        sides = []
+        for rows in segment_rows(f):
             p, q, r = three_parts(rows)
-            seg_side[block, :, i * seg_width : (i + 1) * seg_width] = jnp.concatenate(
-                [p, q, r, p, q, p], axis=0
-            ).astype(BF16)
-        padded = jnp.concatenate([f[3:6], jnp.zeros((5, seg_width), F32)], axis=0)
-        p, q, r = three_parts(padded)
-        normals[block] = jnp.concatenate([p, q], axis=0)
-        return carry
-
-    lax.fori_loop(0, features.shape[0], prepare, 0)
-    out[...] = jnp.zeros(out.shape, F32)
-    count = count_ref[0]
+            stack = jnp.concatenate([p, q, r, p, q, p, jnp.zeros((32, seg_width), F32)], axis=0)
+            sides.append(
+                jnp.concatenate([stack[:, :lanes].T, stack[:, lanes:].T], axis=0).astype(BF16)
+            )
+        for c in range(chunks):
+            for i in range(3):
+                at = (c * 3 + i) * chunk
+                seg_side[block, at : at + chunk, :] = sides[i][c * chunk : (c + 1) * chunk]
+        for i in range(3):
+            pick = (rows128 == i) | (rows128 == 16 + i) | (rows128 == 32 + i)
+            pick = jnp.where(pick, -1.0, 0.0).astype(BF16)
+            normals[block, i] = jnp.dot(sides[0], pick, preferred_element_type=F32)
+        return carry
+
+    lax.fori_loop(0, source_ref.shape[0], prepare, 0)
+    if before is None:
+        out[...] = jnp.zeros(out.shape, F32)
+    else:
+        out[...] = before[...]
+    masked[...] = jnp.zeros(masked.shape, F32)
     per_owner = out.shape[2]
     row = lax.broadcasted_iota(jnp.int32, (8, lanes), 0)
-    by_last = (((1,), (1,)), ((), ()))
-    by_first = (((0,), (0,)), ((), ()))
-
-    def tile_force(t):
-        state = nodes[list_ref[0, t]]
-        block = list_ref[1, t]
+    mask_row = lax.broadcasted_iota(jnp.int32, (32, 2 * lanes), 0)
+    mask_side = lax.broadcasted_iota(jnp.int32, (32, 2 * lanes), 1) // lanes
+
+    def node_side(block):
+        state = nodes[block]
         square = jnp.sum(jnp.where(row < 3, state * state, 0.0), axis=0, keepdims=True)
         extra = jnp.where(row == 0, square, jnp.where(row == 1, 1.0, 0.0))
         p, q, r = three_parts(jnp.concatenate([state, extra], axis=0))
-        node_side = jnp.concatenate([p, p, p, q, q, r], axis=0).astype(BF16)
-        pairs = lax.dot_general(node_side, seg_side[block], by_first, preferred_element_type=F32)
-        magnitude = (
-            jnp.maximum(pairs[:, 0:seg_width], 0.0)
-            * jnp.exp2(pairs[:, seg_width : 2 * seg_width])
-            * pairs[:, 2 * seg_width :]
-        )
-        high = magnitude.astype(BF16)
-        low = (magnitude - high.astype(F32)).astype(BF16)
-        live = jnp.where(t < count, 1.0, 0.0)
-        chosen = (normals[block] * (mask[pl.ds(t, 1), :].astype(F32) * live)).astype(BF16)
-        force = lax.dot_general(
-            chosen, high, by_last, preferred_element_type=F32
-        ) + lax.dot_general(chosen, low, by_last, preferred_element_type=F32)
-        return force[0:8] + force[8:16]
-
-    half = list_ref.shape[1] // 2
-
-    def phase(start, total, add):
-        def turn(index, carry):
-            first = start + index * tiles_per_turn
-            made = [tile_force(first + k) for k in range(tiles_per_turn)]
-            for k, force in enumerate(made):
-                block = list_ref[0, first + k]
-                owner = block // per_owner
-                at = pl.ds(block % per_owner, 1)
-                for f in range(3):
-                    if add:
-                        out[owner, f, at, :] += force[f : f + 1]
-                    else:
-                        out[owner, f, at, :] = force[f : f + 1]
-            return carry
-
-        lax.fori_loop(0, (total + tiles_per_turn - 1) // tiles_per_turn, turn, 0)
-
-    phase(0, jnp.minimum(count, half), False)
-    phase(half, jnp.maximum(count - half, 0), True)
-
-
-def contact_pass(tile_count, tile_list, node_blocks, features, pair_mask, owners):
-    blocks = node_blocks.shape[0]
+        return jnp.concatenate([p, p, p, q, q, r], axis=0)
+
+    def turn(index, carry):
+        pairs = []
+        for k in range(pairs_per_turn):
+            tiles = []
+            for side, listed in enumerate((firsts, seconds)):
+                t = listed[index * pairs_per_turn + k]
+                live = jnp.where(t >= 0, 1.0, 0.0)
+                t = jnp.maximum(t, 0)
+                at = 96 + 2 * k + side
+                masked[at : at + 1, :] = 1.0 - mask[pl.ds(t, 1), :].astype(F32) * live
+                tiles.append(t)
+            block = jnp.clip(list_ref[1, tiles[0]] - first_block, 0, source_ref.shape[0] - 1)
+            pairs.append((list_ref[0, tiles[0]], list_ref[0, tiles[1]], block))
+        hidden = jnp.concatenate([masked[:, :lanes].T, masked[:, lanes:].T], axis=0).astype(BF16)
+        forces = []
+        for k, (one, two, block) in enumerate(pairs):
+            both = jnp.concatenate([node_side(one), node_side(two)], axis=1)
+            away = jnp.where(mask_row == 2 * k + mask_side, -mask_power, 0.0)
+            weights = jnp.concatenate([both, away], axis=0).astype(BF16)
+            parts = []
+            for c in range(chunks):
+                at = c * 3 * chunk
+                parts.append(seg_side[block, at : at + chunk, :])
+                parts.append(
+                    seg_side[block, at + chunk : at + 2 * chunk, :]
+                    + hidden[c * chunk : (c + 1) * chunk]
+                )
+                parts.append(seg_side[block, at + 2 * chunk : at + 3 * chunk, :])
+            terms = jnp.dot(
+                jnp.concatenate(parts, axis=0), weights, preferred_element_type=F32
+            )
+            sums = [[None] * 3, [None] * 3]
+            for c in range(chunks):
+                for h in range(chunk // 8):
+                    at = c * 3 * chunk + h * 8
+                    seg = c * chunk + h * 8
+                    normal = [normals[block, i, seg : seg + 8, :] for i in range(3)]
+                    for side in range(2):
+                        cols = slice(side * lanes, (side + 1) * lanes)
+                        magnitude = (
+                            jnp.maximum(terms[at : at + 8, cols], 0.0)
+                            * jnp.exp2(terms[at + chunk : at + chunk + 8, cols])
+                            * terms[at + 2 * chunk : at + 2 * chunk + 8, cols]
+                        )
+                        for i in range(3):
+                            part = magnitude * normal[i]
+                            old = sums[side][i]
+                            sums[side][i] = part if old is None else old + part
+            forces.append(
+                [[jnp.sum(part, axis=0, keepdims=True) for part in sums[side]] for side in range(2)]
+            )
+        for k, (one, two, _) in enumerate(pairs):
+            for side, block in enumerate((one, two)):
+                for i in range(3):
+                    out[block // per_owner, i, pl.ds(block % per_owner, 1), :] += forces[k][side][i]
+        return carry
+
+    turns = (total_ref[0] + pairs_per_turn - 1) // pairs_per_turn
+    lax.fori_loop(0, turns, turn, 0)
+
+
+def contact_pass(
+    first_block, total, firsts, seconds, tile_list, sources, live,
+    node_blocks, features, pair_mask, owners, before,
+):
+    per_owner = node_blocks.shape[0] // owners
+    seg_blocks = sources.shape[0]
+    first_call = before is None
+
+    def kernel(*refs):
+        refs = list(refs)
+        if first_call:
+            refs.insert(9, None)
+        contact_kernel(first_block, *refs)
+
+    operands = [total, firsts, seconds, tile_list, sources, live, node_blocks, features, pair_mask]
+    specs = [in_smem] * 6 + [in_vmem] * 3
+    if not first_call:
+        operands.append(before)
+        specs.append(in_vmem)
     return pl.pallas_call(
-        contact_kernel,
-        out_shape=jax.ShapeDtypeStruct((owners, 3, blocks // owners, lanes), F32),
-        in_specs=[in_smem, in_smem, in_vmem, in_vmem, in_vmem],
+        kernel,
+        out_shape=jax.ShapeDtypeStruct((owners, 3, per_owner, lanes), F32),
+        in_specs=specs,
         out_specs=in_vmem,
         scratch_shapes=[
-            pltpu.VMEM((features.shape[0], 96, 3 * seg_width), BF16),
-            pltpu.VMEM((features.shape[0], 16, seg_width), F32),
+            pltpu.VMEM((seg_blocks, 3 * seg_width, lanes), BF16),
+            pltpu.VMEM((seg_blocks, 3, seg_width, lanes), F32),
+            pltpu.VMEM((lanes, seg_width), F32),
         ],
         compiler_params=pltpu.CompilerParams(vmem_limit_bytes=vmem_limit),
-    )(tile_count, tile_list, node_blocks, features, pair_mask)
-
-
-def with_neighbours(cells, axis):
-    count = lax.axis_size(axis)
-    up = [(i, i + 1) for i in range(count - 1)]
-    down = [(i + 1, i) for i in range(count - 1)]
-    return jnp.stack([lax.ppermute(cells, axis, up), cells, lax.ppermute(cells, axis, down)])
+    )(*operands)
+
+
+def ghost_sources(edge):
+    rows, columns = lax.axis_size("wide"), lax.axis_size("narrow")
+    a, b = lax.axis_index("wide"), lax.axis_index("narrow")
+    sources, live = [], []
+    for da in (-1, 0, 1):
+        for db in (-1, 0, 1):
+            if (da, db) == (0, 0):
+                continue
+            inside = (a + da >= 0) & (a + da < rows) & (b + db >= 0) & (b + db < columns)
+            cell = jnp.where(inside, (a + da) * columns + b + db, 0)
+            for e in range(edge):
+                sources.append(cell * edge + e)
+                live.append(inside.astype(jnp.int32))
+    return jnp.stack(sources).astype(jnp.int32), jnp.stack(live)
 
 
 def on_device(
@@ -344,12 +475,23 @@
     arrived = lax.all_to_all(
         outgoing.reshape(owners, per_owner, 8, lanes), both, split_axis=0, concat_axis=0
     ).reshape(-1, 8, lanes)
-    own = segment_features(connectivity.T, arrived)
-    edge = connectivity.shape[0] // 4 // seg_width
-    rim = with_neighbours(with_neighbours(own[:edge], "wide"), "narrow")
-    ghosts = [rim[db, da] for da in range(3) for db in range(3) if (da, db) != (1, 1)]
-    features = jnp.concatenate([own] + ghosts, axis=0)
-    slot_force = contact_pass(tile_count, tile_list, arrived, features, pair_mask, owners)
+    own_blocks = connectivity.shape[0] // seg_width
+    edge = own_blocks // 4
+    total, first_own, second_own, first_far, second_far = tile_pairs(
+        tile_count, tile_list, own_blocks, own_blocks + 8 * edge
+    )
+    own = segment_features(connectivity, arrived)
+    edges = lax.all_gather(own[:edge], both, axis=0, tiled=True)
+    sources, live = ghost_sources(edge)
+    slot_force = contact_pass(
+        0, total[0:1], first_own, second_own, tile_list,
+        jnp.arange(own_blocks, dtype=jnp.int32), jnp.ones((own_blocks,), jnp.int32),
+        arrived, own, pair_mask, owners, None,
+    )
+    slot_force = contact_pass(
+        own_blocks, total[1:2], first_far, second_far, tile_list,
+        sources, live, arrived, edges, pair_mask, owners, slot_force,
+    )
     returned = lax.all_to_all(slot_force, both, split_axis=0, concat_axis=0)
     forces = jnp.transpose(returned, (1, 0, 2, 3)).reshape(3, -1, lanes)
     return unpack(slots_row, forces, positions.shape[1])

time: 502 us -> 345 us (0.69)
  blocking collectives: 263 us -> 48.1 us
  waiting for transfers between devices: 7.44 us -> 67.3 us
  Pallas kernels: 214 us -> 190 us
  between operations: 0.78 us -> 14.2 us
    all_to_all x1, blocking collectives: 207 us -> 48.1 us  [on_device(): returned = lax.all_to_all(slot_force, both, split_axis=0, concat_axis=0)]
    all_to_all x1 -> x0, blocking collectives: 56.1 us -> none  [on_device(): lax.all_to_all(outgoing.reshape(owners, per_owner, 8, lanes), both, split...]
    all_to_all x0 -> x1, waiting for transfers between devices: none -> 47.4 us  [on_device(): lax.all_to_all(outgoing.reshape(owners, per_owner, 8, lanes), both, split...]
    pallas_call x2 -> x4, Pallas kernels: 105 us -> 81.3 us  [the longest x2 52.9 us: contact_pass(): pl.pallas_call(kernel, out_shape=jax.ShapeDtypeStruct((owners, 3, per_own...]
    all_gather x0 -> x1, waiting for transfers between devices: none -> 19.9 us  [on_device(): edges = lax.all_gather(own[:edge], both, axis=0, tiled=True)]
    ppermute x4 -> x0, waiting for transfers between devices: 7.44 us -> none  [the longest x2 7.43 us: with_neighbours(): lax.ppermute(cells, axis, down)]
    all_to_all x0 -> x1, starting transfers between devices: none -> 7.31 us  [on_device(): lax.all_to_all(outgoing.reshape(owners, per_owner, 8, lanes), both, split...]
    ppermute x4 -> x0, starting transfers between devices: 7.24 us -> none  [the longest x2 4.65 us: with_neighbours(): lax.ppermute(cells, axis, up)]
  transfers between devices with their start and end apart: 4 -> 2, of which waited for: 2 -> 2; matrix products, arithmetic and copies ran while one was open for 0% -> 1% of each run, Pallas kernels for 0% -> 9%
where the time goes in v2:
time: 345 us; the launch traced here: 339 us
  Pallas kernels  190 us (55%)
  waiting for transfers between devices  67.3 us (20%)
  blocking collectives  48.1 us (14%)
  between operations  14.2 us (4%)
  local copies, waits for them, and re-layouts  7.45 us (2%)
  starting transfers between devices  7.35 us (2%)
  other arithmetic  4.69 us (1%)
    pallas_call x1, Pallas kernels, unpack(): pl.pallas_call(unpack_kernel, out_shape=jax.ShapeDtypeStruct((3, count),...  54.9 us
    pallas_call x1, Pallas kernels, pack(): pl.pallas_call(pack_kernel, out_shape=jax.ShapeDtypeStruct((slots_row.sha...  54.2 us
    pallas_call x2, Pallas kernels, contact_pass(): pl.pallas_call(kernel, out_shape=jax.ShapeDtypeStruct((owners, 3, per_own...  52.9 us
    all_to_all x1, blocking collectives, on_device(): returned = lax.all_to_all(slot_force, both, split_axis=0, concat_axis=0)  48.1 us
    all_to_all x1, waiting for transfers between devices, on_device(): lax.all_to_all(outgoing.reshape(owners, per_owner, 8, lanes), both, split...  47.4 us
    all_gather x1, waiting for transfers between devices, on_device(): edges = lax.all_gather(own[:edge], both, axis=0, tiled=True)  19.9 us
    pallas_call x1, Pallas kernels, segment_features(): pl.pallas_call(feature_kernel, out_shape=jax.ShapeDtypeStruct((quads // s...  17.9 us
    pallas_call x1, Pallas kernels, tile_pairs(): pl.pallas_call(partial(pair_kernel, own_blocks), out_shape=[jax.ShapeDtyp...  10.5 us
  transfers between devices with their start and end apart: 2, of which 2 were waited for; matrix products, arithmetic and copies ran while one was open for 1% of the time, Pallas kernels for 9%

profile of v2, /device:TPU:0, one launch (start us, length us, event | category | flops | bytes accessed | tf_op | source)
XLA Modules:
  0.0 339.5 jit_solution(13447746027344548516)
XLA Ops:
  6.5 3.4 %pad_maximum_fusion.nodes = f32[8,49152]{1,0:T(8,128)} fusion(f32[1,49152]{1,0:T(1,128)} %bitcast.67, f32[1,49152]{1,0:T(1,128)} %bitcast.68, f32[3,49152]{1,0:T(4,128)} %param.10, f32[3,49152]{1,0:T(4,128)} %param.9), kind=kLoop, calls=%fused_computation | loop fusion | flops 1179648 | bytes 3145728 | tf_op jit(solution)/shard_map/concatenate | solution.py:471
  10.0 54.2 %shard_map.92 = f32[512,8,128]{2,1,0:T(8,128)} custom-call(s32[65536]{0:T(1024)} %bitcast.65, f32[8,49152]{1,0:T(8,128)} %pad_maximum_fusion.nodes), custom_call_target="tpu_custom_call" | custom-call | tf_op jit(solution)/shard_map/pallas_call | solution.py:89
  64.2 0.0 copy-start.1
  64.2 7.3 %all-to-all-start = ((f32[32,16,8,128]{3,2,1,0:T(8,128)}), f32[32,16,8,128]{3,2,1,0:T(8,128)S(1)}, u32[]{:S(2)}, u32[]{:S(2)}) async-start(f32[32,16,8,128]{3,2,1,0:T(8,128)} %bitcast.62), calls=%async_computation | async-start | bytes 4194304 | tf_op jit(solution)/shard_map/all_to_all | solution.py:475
  71.5 0.0 all-gather.2.cloned.1.call-start
  71.5 0.0 copy-done.1
  71.5 0.7 fusion.1
  72.2 0.6 copy.14
  72.8 47.4 %all-to-all-done = f32[32,16,8,128]{3,2,1,0:T(8,128)S(1)} async-done(((f32[32,16,8,128]{3,2,1,0:T(8,128)}), f32[32,16,8,128]{3,2,1,0:T(8,128)S(1)}, u32[]{:S(2)}, u32[]{:S(2)}) %all-to-all-start) | async-done | bytes 2097184 | tf_op jit(solution)/shard_map/all_to_all | solution.py:475
  120.3 0.0 copy-start
  120.3 1.3 copy-done
  121.6 17.9 %shard_map.93.refs_7_ = f32[8,16,256]{2,1,0:T(8,128)} custom-call(s32[4,2048]{1,0:T(4,128)} %get-tuple-element.16.start_ref, f32[4096,128]{1,0:T(8,128)} %bitcast.59, s32[4,16,128]{2,1,0:T(8,128)} %bitcast.69), custom_call_target="tpu_custom_call" | custom-call | tf_op jit(solution)/shard_map/pallas_call | solution.py:213
  139.5 1.4 slice.12
  140.8 0.0 all-gather.2.cloned.1.call-update
  141.6 0.1 stack.121
  141.7 0.6 stack.122.refs_5_
  142.3 10.5 %shard_map.91 = (s32[2]{0:T(128)}, s32[640]{0:T(1024)}, s32[640]{0:T(1024)}, s32[640]{0:T(1024)}, s32[640]{0:T(1024)}) custom-call(s32[1]{0:T(128)S(6)} %copy.15.count_ref, s32[2,1024]{1,0:T(2,128)} %refs_3_.3), custom_call_target="tpu_custom_call" | custom-call | tf_op jit(solution)/shard_map/pallas_call | solution.py:294
  152.8 0.7 stack.112.refs_4_
  153.5 1.3 fusion.4
  154.8 0.5 iota.3.refs_4_
  155.3 0.5 broadcast_3_refs_5_.2.refs_5_
  155.8 18.7 %shard_map.94.refs_9_ = f32[32,3,16,128]{3,2,1,0:T(8,128)} custom-call(s32[1]{0:T(128)} %get-tuple-element.17.refs_0_, s32[640]{0:T(1024)} %get-tuple-element.13.refs_1_, s32[640]{0:T(1024)} %get-tuple-element.14.refs_2_, s32[2,1024]{1,0:T(2,128)} %refs_3_.3, s32[8]{0:T(128)} %iota.3.refs_4_, s32[8]{0:T(128)} %broadcast_3_refs_5_.2.refs_5_, ...), custom_call_target="tpu_custom_call" | custom-call | tf_op jit(solution)/shard_map/pallas_call | solution.py:428
  174.5 19.9 %all-gather.2.cloned.1.call-done.refs_7_ = f32[64,16,256]{2,1,0:T(8,128)} async-done(((f32[2,16,256]{2,1,0:T(8,128)}), f32[64,16,256]{2,1,0:T(8,128)}) %all-gather.2.cloned.1.call-update) | async-done | bytes 1048592 | tf_op jit(solution)/shard_map/all_gather | solution.py:484
  194.4 34.3 %shard_map.95 = f32[32,3,16,128]{3,2,1,0:T(8,128)} custom-call(s32[1]{0:T(128)} %get-tuple-element.18.refs_0_, s32[640]{0:T(1024)} %get-tuple-element.11.refs_1_, s32[640]{0:T(1024)} %get-tuple-element.12.refs_2_, s32[2,1024]{1,0:T(2,128)} %refs_3_.3, s32[16]{0:T(128)} %stack.112.refs_4_, s32[16]{0:T(128)} %stack.122.refs_5_, f32[512,8,128]{2,1,0:T(8,128)} %bitcast.61, ...), custom_call_target="tpu_custom_call" | custom-call | tf_op jit(solution)/shard_map/pallas_call | solution.py:428
  228.6 48.1 %all_to_all.10 = f32[32,3,16,128]{3,2,1,0:T(8,128)S(1)} all-to-all(f32[32,3,16,128]{3,2,1,0:T(8,128)} %shard_map.95), channel_id=1, replica_groups=mesh['wide'=8,'narrow'=4] {'wide','narrow'}, dimensions={0} | all-to-all | bytes 1572864 | tf_op jit(solution)/shard_map/all_to_all | solution.py:495
  276.7 0.9 copy.11
  277.7 54.9 %shard_map.96 = f32[3,49152]{1,0:T(4,128)} custom-call(s32[65536]{0:T(1024)} %bitcast.66, f32[3,512,128]{2,1,0:T(8,128)} %bitcast.63), custom_call_target="tpu_custom_call" | custom-call | tf_op jit(solution)/shard_map/pallas_call | solution.py:145
Async XLA Ops:
  64.2 7.4 %copy-start.1 = (s32[2048,4]{0,1:T(4,128)S(1)}, s32[2048,4]{0,1:T(4,128)}, u32[]{:S(2)}) copy-start(s32[2048,4]{0,1:T(4,128)} %param.14) | copy-start | bytes 98308
  64.2 56.1 %all-to-all-start = ((f32[32,16,8,128]{3,2,1,0:T(8,128)}), f32[32,16,8,128]{3,2,1,0:T(8,128)S(1)}, u32[]{:S(2)}, u32[]{:S(2)}) async-start(f32[32,16,8,128]{3,2,1,0:T(8,128)} %bitcast.62), calls=%async_computation | async-start | bytes 4194304 | tf_op jit(solution)/shard_map/all_to_all | solution.py:475
  71.5 122.9 %all-gather.2.cloned.1.call-start = ((), (), s32[]{:S(2)}) async-start(), calls=%async_computation.2 | async-start | bytes 1081344 | tf_op jit(solution)/shard_map/all_gather | solution.py:484
  120.3 1.3 copy-start
Sparse Core Ops, SparseCore 0:
  141.0 53.3 all-gather.1

commit v3 on v2

v3 whole, which is shorter than its diff:
```python
import math
from functools import partial

import jax
import jax.numpy as jnp
from jax import lax
from jax.experimental import pallas as pl
from jax.experimental.pallas import tpu as pltpu
from jax.sharding import PartitionSpec as P

stiffness = 1.0
damping = 0.3
lanes = 128
groups = 16
span = lanes * groups
half_span = span // 2
seg_width = 256
table_unroll = 4
pairs_per_turn = 16
mask_power = 256.0
vmem_limit = 60 * 2**20
F32 = jnp.float32
BF16 = jnp.bfloat16
in_vmem = pl.BlockSpec(memory_space=pltpu.VMEM)
in_smem = pl.BlockSpec(memory_space=pltpu.SMEM)
in_hbm = pl.BlockSpec(memory_space=pl.ANY)


def pack_kernel(
    first, blocks, per_owner, index_ref, nodes, out, table, rows, parts, buffer_a, buffer_b, sems
):
    count = nodes.shape[1]
    supers = count // span
    buffers = (buffer_a, buffer_b)
    turns = out.shape[0] // groups
    piece = math.gcd(blocks * lanes, half_span)
    pieces = half_span // piece
    owner_pieces = blocks * lanes // piece

    def fetch(turn, part):
        copies = []
        for k in range(pieces):
            number = (turn * 2 + part) * pieces + k
            start = (number // owner_pieces * per_owner + first) * lanes
            start = start + number % owner_pieces * piece
            copies.append(
                pltpu.make_async_copy(
                    index_ref.at[pl.ds(pl.multiple_of(start, piece), piece)],
                    buffers[part].at[pl.ds(k * piece, piece)],
                    sems.at[part, k],
                )
            )
        return copies

    for part in range(2):
        for copy in fetch(0, part):
            copy.start()

    def turn_around(step, carry):
        for i in range(table_unroll):
            number = step * table_unroll + i
            states = nodes[:, pl.ds(pl.multiple_of(number * span, span), span)]
            stacked = jnp.concatenate(
                [states[:, g * lanes : (g + 1) * lanes] for g in range(groups)], axis=0
            )
            at = pl.ds(pl.multiple_of(number * lanes, lanes), lanes)
            for k, part in enumerate(three_parts(stacked.T)):
                parts[at, k * lanes : (k + 1) * lanes] = part.astype(BF16)
        return carry

    lax.fori_loop(0, supers // table_unroll, turn_around, 0)
    source = lax.broadcasted_iota(jnp.int32, (3 * lanes, 2 * lanes), 0) % lanes
    target = lax.broadcasted_iota(jnp.int32, (3 * lanes, 2 * lanes), 1)

    def spread(pair, carry):
        wanted = (2 * pair + target // lanes) * 8 + target % 8
        pick = jnp.where(source == wanted, 1.0, 0.0).astype(BF16)
        for step in range(supers // table_unroll):
            height = table_unroll * lanes
            wide = jnp.dot(
                parts[step * height : (step + 1) * height, :], pick, preferred_element_type=F32
            )
            for i in range(table_unroll):
                start = (step * table_unroll + i) * span + pair * 2 * lanes
                start = pl.multiple_of(start, 2 * lanes)
                for side in range(2):
                    table[pl.ds(start + side * lanes, lanes), :] = wide[
                        i * lanes : (i + 1) * lanes, side * lanes : (side + 1) * lanes
                    ]
        return carry

    lax.fori_loop(0, groups // 2, spread, 0)
    table[count : count + 8, :] = jnp.zeros((8, lanes), F32)

    def body(turn, carry):
        for part in range(2):
            for copy in fetch(turn, part):
                copy.wait()
            for j in range(lanes):
                for i in range(groups // 2):
                    cols = slice((part * groups // 2 + i) * 8, (part * groups // 2 + i + 1) * 8)
                    row = buffers[part][i * lanes + j]
                    rows[j : j + 1, cols] = table[pl.ds(row, 1), cols]

            @pl.when(turn + 1 < turns)
            def _():
                for copy in fetch(turn + 1, part):
                    copy.start()

        out[pl.ds(turn * groups, groups)] = rows[...].T.reshape(groups, 8, lanes)
        return carry

    lax.fori_loop(0, turns, body, 0)


def pack(slots_row, node_data, owners, first, blocks):
    per_owner = slots_row.shape[0] // lanes // owners
    count = node_data.shape[1]
    return pl.pallas_call(
        partial(pack_kernel, first, blocks, per_owner),
        out_shape=jax.ShapeDtypeStruct((owners * blocks, 8, lanes), F32),
        in_specs=[in_hbm, in_vmem],
        out_specs=in_vmem,
        scratch_shapes=[
            pltpu.VMEM((count + 8, lanes), F32),
            pltpu.VMEM((lanes, lanes), F32),
            pltpu.VMEM((count // groups, 3 * lanes), BF16),
            pltpu.SMEM((half_span,), jnp.int32),
            pltpu.SMEM((half_span,), jnp.int32),
            pltpu.SemaphoreType.DMA((2, half_span // math.gcd(blocks * lanes, half_span))),
        ],
        compiler_params=pltpu.CompilerParams(vmem_limit_bytes=vmem_limit),
    )(slots_row, node_data)


def quad_features(corners):
    x = [c[0:3] for c in corners]
    v = [c[3:6] for c in corners]
    centre = (x[0] + x[1] + x[2] + x[3]) * 0.25
    a = x[2] - x[0]
    b = x[3] - x[1]
    cross = jnp.concatenate(
        [
            a[1:2] * b[2:3] - a[2:3] * b[1:2],
            a[2:3] * b[0:1] - a[0:1] * b[2:3],
            a[0:1] * b[1:2] - a[1:2] * b[0:1],
        ],
        axis=0,
    )
    length = jnp.sqrt(jnp.sum(cross * cross, axis=0, keepdims=True))
    normal = cross / jnp.maximum(length, 1.0)
    drift = (v[0] + v[1] + v[2] + v[3]) * 0.25
    apart = sum((xi - centre) ** 2 for xi in x)
    spread = jnp.sum(apart, axis=0, keepdims=True) * 0.25
    return jnp.concatenate(
        [centre, normal, drift, spread, jnp.zeros((6, lanes), F32)], axis=0
    )


def load_halves(halves, nodes, sems):
    copies = []
    filled = 0
    for i, half in enumerate(halves):
        blocks = half.shape[1]
        copies.append(pltpu.make_async_copy(half, nodes.at[:, pl.ds(filled, blocks)], sems.at[i]))
        filled += blocks
    for copy in copies:
        copy.start()
    return copies


def feature_kernel(start_ref, half_a, half_b, place, out, nodes, buffer_a, buffer_b, sems, half_sems):
    lane = lax.broadcasted_iota(jnp.int32, (8, lanes), 1)
    flat = nodes.reshape(nodes.shape[0] * nodes.shape[1] * 8, lanes)
    buffers = (buffer_a, buffer_b)
    size = 4 * lanes

    def fetch(block, part):
        start = pl.multiple_of(block * size, size)
        return pltpu.make_async_copy(start_ref.at[pl.ds(start, size)], buffers[part], sems.at[part])

    for part in range(2):
        fetch(part, part).start()
    for copy in load_halves((half_a, half_b), nodes, half_sems):
        copy.wait()
    pairs = place.shape[1] // 2

    def body(pair, carry):
        for part in range(2):
            block = pair * 2 + part
            fetch(block, part).wait()
            corners = []
            for i in range(4):
                where = jnp.broadcast_to(place[i, pl.ds(block, 1), :], (8, lanes))
                state = jnp.zeros((8, lanes), F32)
                for j in range(lanes):
                    start = pl.multiple_of(buffers[part][i * lanes + j], 8)
                    moved = jnp.take_along_axis(flat[pl.ds(start, 8), :], where, axis=1)
                    state = jnp.where(lane == j, moved, state)
                corners.append(state)

            @pl.when(pair + 1 < pairs)
            def _():
                fetch(block + 2, part).start()

            out[pair, :, part * lanes : (part + 1) * lanes] = quad_features(corners)
        return carry

    lax.fori_loop(0, pairs, body, 0)


def segment_features(corner_slots, half_a, half_b):
    quads = corner_slots.shape[0]
    by_block = jnp.transpose(corner_slots.reshape(-1, lanes, 4), (0, 2, 1))
    owners = half_a.shape[0]
    per_owner = half_a.shape[1] + half_b.shape[1]
    return pl.pallas_call(
        feature_kernel,
        out_shape=jax.ShapeDtypeStruct((quads // seg_width, 16, seg_width), F32),
        in_specs=[in_hbm, in_hbm, in_hbm, in_vmem],
        out_specs=in_vmem,
        scratch_shapes=[
            pltpu.VMEM((owners, per_owner, 8, lanes), F32),
            pltpu.SMEM((4 * lanes,), jnp.int32),
            pltpu.SMEM((4 * lanes,), jnp.int32),
            pltpu.SemaphoreType.DMA((2,)),
            pltpu.SemaphoreType.DMA((2,)),
        ],
        compiler_params=pltpu.CompilerParams(vmem_limit_bytes=vmem_limit),
    )(
        (by_block // lanes * 8).reshape(-1),
        half_a,
        half_b,
        jnp.transpose(by_block % lanes, (1, 0, 2)),
    )


def three_parts(x):
    first = x.astype(BF16).astype(F32)
    rest = x - first
    second = rest.astype(BF16).astype(F32)
    return first, second, rest - second


def segment_rows(f):
    centre, normal, drift, spread = f[0:3], f[3:6], f[6:9], f[9:10]
    zero = jnp.zeros_like(spread)
    one = jnp.ones_like(spread)
    zeros = jnp.zeros_like(centre)
    rate = math.log2(math.e) / (spread + 0.25)
    plane = jnp.sum(centre * normal, axis=0, keepdims=True)
    square = jnp.sum(centre * centre, axis=0, keepdims=True)
    slide = jnp.sum(drift * normal, axis=0, keepdims=True)
    depth = [-normal, zeros, zero, one, zero, plane, zeros, zeros]
    power = [(2.0 * rate) * centre, zeros, zero, zero, -rate, -(rate * square), zeros, zeros]
    push = [zeros, -damping * normal, stiffness * one, zero, zero, damping * slide, zeros, zeros]
    return [jnp.concatenate(rows, axis=0) for rows in (depth, power, push)]


def pair_kernel(
    own_blocks, count_ref, list_ref, total, first_own, second_own, first_far, second_far, waiting
):
    blocks = waiting.shape[0]
    for block in range(blocks):
        waiting[block] = -1

    def match(t, counts):
        own_count, far_count = counts
        block = list_ref[1, t]
        other = waiting[block]
        met = (other >= 0).astype(jnp.int32)
        first_own[own_count] = other
        second_own[own_count] = t
        first_far[far_count] = other
        second_far[far_count] = t
        waiting[block] = jnp.where(other >= 0, -1, t)
        is_own = block < own_blocks
        return own_count + jnp.where(is_own, met, 0), far_count + jnp.where(is_own, 0, met)

    own_count, far_count = lax.fori_loop(0, count_ref[0], match, (jnp.int32(0), jnp.int32(0)))

    def leave(first, second):
        def step(block, count):
            other = waiting[block]
            first[count] = other
            second[count] = -1
            return count + (other >= 0).astype(jnp.int32)

        return step

    own_count = lax.fori_loop(0, own_blocks, leave(first_own, second_own), own_count)
    far_count = lax.fori_loop(own_blocks, blocks, leave(first_far, second_far), far_count)
    for k in range(pairs_per_turn):
        first_own[own_count + k] = -1
        second_own[own_count + k] = -1
        first_far[far_count + k] = -1
        second_far[far_count + k] = -1
    total[0] = own_count
    total[1] = far_count


def tile_pairs(tile_count, tile_list, own_blocks, blocks):
    room = tile_list.shape[1] // 2 + blocks + pairs_per_turn
    room = (room + lanes - 1) // lanes * lanes
    listed = jax.ShapeDtypeStruct((room,), jnp.int32)
    return pl.pallas_call(
        partial(pair_kernel, own_blocks),
        out_shape=[jax.ShapeDtypeStruct((2,), jnp.int32)] + [listed] * 4,
        in_specs=[in_smem, in_smem],
        out_specs=[in_smem] * 5,
        scratch_shapes=[pltpu.SMEM((blocks,), jnp.int32)],
    )(tile_count, tile_list)


def contact_kernel(
    first_block, plan, part_refs, total_ref, firsts, seconds, list_ref,
    half_a, half_b, mask, before, out, features, seg_side, normals, masked, nodes, half_sems,
):
    node_copies = load_halves((half_a, half_b), nodes, half_sems)
    filled = 0
    for which, at in plan:
        part = part_refs[which] if at is None else part_refs[which].at[at]
        features[filled : filled + part.shape[0]] = part[...]
        filled += part.shape[0]
    rows128 = lax.broadcasted_iota(jnp.int32, (lanes, lanes), 0)
    chunk = 16
    chunks = seg_width // chunk

    def prepare(block):
        f = features[block]
        sides = []
        for rows in segment_rows(f):
            p, q, r = three_parts(rows)
            stack = jnp.concatenate([p, q, r, p, q, p, jnp.zeros((32, seg_width), F32)], axis=0)
            sides.append(
                jnp.concatenate([stack[:, :lanes].T, stack[:, lanes:].T], axis=0).astype(BF16)
            )
        for c in range(chunks):
            for i in range(3):
                at = (c * 3 + i) * chunk
                seg_side[block, at : at + chunk, :] = sides[i][c * chunk : (c + 1) * chunk]
        for i in range(3):
            pick = (rows128 == i) | (rows128 == 16 + i) | (rows128 == 32 + i)
            pick = jnp.where(pick, -1.0, 0.0).astype(BF16)
            normals[block, i] = jnp.dot(sides[0], pick, preferred_element_type=F32)

    def prepare_some(step, carry):
        for i in range(together):
            prepare(step * together + i)
        return carry

    together = math.gcd(features.shape[0], 4)
    lax.fori_loop(0, features.shape[0] // together, prepare_some, 0)
    if before is None:
        out[...] = jnp.zeros(out.shape, F32)
    else:
        out[...] = before[...]
    masked[...] = jnp.zeros(masked.shape, F32)
    per_owner = out.shape[2]
    for copy in node_copies:
        copy.wait()
    row = lax.broadcasted_iota(jnp.int32, (8, lanes), 0)
    mask_row = lax.broadcasted_iota(jnp.int32, (32, 2 * lanes), 0)
    mask_side = lax.broadcasted_iota(jnp.int32, (32, 2 * lanes), 1) // lanes

    def node_side(block):
        state = nodes[block // per_owner, block % per_owner]
        square = jnp.sum(jnp.where(row < 3, state * state, 0.0), axis=0, keepdims=True)
        extra = jnp.where(row == 0, square, jnp.where(row == 1, 1.0, 0.0))
        p, q, r = three_parts(jnp.concatenate([state, extra], axis=0))
        return jnp.concatenate([p, p, p, q, q, r], axis=0)

    def turn(index, carry):
        pairs = []
        for k in range(pairs_per_turn):
            tiles = []
            for side, listed in enumerate((firsts, seconds)):
                t = listed[index * pairs_per_turn + k]
                live = jnp.where(t >= 0, 1.0, 0.0)
                t = jnp.maximum(t, 0)
                at = 96 + 2 * k + side
                masked[at : at + 1, :] = 1.0 - mask[pl.ds(t, 1), :].astype(F32) * live
                tiles.append(t)
            block = jnp.clip(list_ref[1, tiles[0]] - first_block, 0, features.shape[0] - 1)
            pairs.append((list_ref[0, tiles[0]], list_ref[0, tiles[1]], block))
        hidden = jnp.concatenate([masked[:, :lanes].T, masked[:, lanes:].T], axis=0).astype(BF16)
        forces = []
        for k, (one, two, block) in enumerate(pairs):
            both = jnp.concatenate([node_side(one), node_side(two)], axis=1)
            away = jnp.where(mask_row == 2 * k + mask_side, -mask_power, 0.0)
            weights = jnp.concatenate([both, away], axis=0).astype(BF16)
            parts = []
            for c in range(chunks):
                at = c * 3 * chunk
                parts.append(seg_side[block, at : at + chunk, :])
                parts.append(
                    seg_side[block, at + chunk : at + 2 * chunk, :]
                    + hidden[c * chunk : (c + 1) * chunk]
                )
                parts.append(seg_side[block, at + 2 * chunk : at + 3 * chunk, :])
            terms = jnp.dot(
                jnp.concatenate(parts, axis=0), weights, preferred_element_type=F32
            )
            sums = [[None] * 3, [None] * 3]
            for c in range(chunks):
                at = c * 3 * chunk
                magnitude = (
                    jnp.maximum(terms[at : at + chunk], 0.0)
                    * jnp.exp2(terms[at + chunk : at + 2 * chunk])
                    * terms[at + 2 * chunk : at + 3 * chunk]
                )
                normal = [normals[block, i, c * chunk : (c + 1) * chunk, :] for i in range(3)]
                for side in range(2):
                    half = magnitude[:, side * lanes : (side + 1) * lanes]
                    for i in range(3):
                        part = half * normal[i]
                        old = sums[side][i]
                        sums[side][i] = part if old is None else old + part
            forces.append(
                [[jnp.sum(part, axis=0, keepdims=True) for part in sums[side]] for side in range(2)]
            )
        for k, (one, two, _) in enumerate(pairs):
            for side, block in enumerate((one, two)):
                for i in range(3):
                    out[block // per_owner, i, pl.ds(block % per_owner, 1), :] += forces[k][side][i]
        return carry

    turns = (total_ref[0] + pairs_per_turn - 1) // pairs_per_turn
    lax.fori_loop(0, turns, turn, 0)


def contact_pass(
    first_block, total, firsts, seconds, tile_list, half_a, half_b, pair_mask, parts, plan, before
):
    owners = half_a.shape[0]
    per_owner = half_a.shape[1] + half_b.shape[1]
    seg_blocks = sum(parts[which].shape[0 if at is None else 1] for which, at in plan)
    first_call = before is None

    def kernel(*refs):
        refs = list(refs)
        part_refs, rest = refs[: len(parts)], refs[len(parts) :]
        if first_call:
            rest.insert(7, None)
        contact_kernel(first_block, plan, part_refs, *rest)

    operands = [*parts, total, firsts, seconds, tile_list, half_a, half_b, pair_mask]
    specs = [in_vmem] * len(parts) + [in_smem] * 4 + [in_hbm] * 2 + [in_vmem]
    if not first_call:
        operands.append(before)
        specs.append(in_vmem)
    return pl.pallas_call(
        kernel,
        out_shape=jax.ShapeDtypeStruct((owners, 3, per_owner, lanes), F32),
        in_specs=specs,
        out_specs=in_vmem,
        scratch_shapes=[
            pltpu.VMEM((seg_blocks, 16, seg_width), F32),
            pltpu.VMEM((seg_blocks, 3 * seg_width, lanes), BF16),
            pltpu.VMEM((seg_blocks, 3, seg_width, lanes), F32),
            pltpu.VMEM((lanes, seg_width), F32),
            pltpu.VMEM((owners, per_owner, 8, lanes), F32),
            pltpu.SemaphoreType.DMA((2,)),
        ],
        compiler_params=pltpu.CompilerParams(vmem_limit_bytes=vmem_limit),
    )(*operands)


def with_neighbours(cells, axis):
    ends = lax.axis_size(axis) - 1
    before = lax.ppermute(cells, axis, [(i, i + 1) for i in range(ends)])
    after = lax.ppermute(cells, axis, [(i + 1, i) for i in range(ends)])
    return before, cells, after


def sort_kernel(keys, values, out, key_s, *value_s):
    high, low = key_s.shape[:2]
    low_bits, high_bits = low.bit_length() - 1, high.bit_length() - 1
    vector_bits = low_bits + high_bits
    total_bits = vector_bits + 10
    refs = (key_s, *value_s)
    lane = lax.broadcasted_iota(jnp.int32, (8, lanes), 1)
    sub = lax.broadcasted_iota(jnp.int32, (8, lanes), 0)
    inside = (lane * 8 + sub) << vector_bits
    wide = (low, 8, lanes)
    lane_w = lax.broadcasted_iota(jnp.int32, wide, 2)
    sub_w = lax.broadcasted_iota(jnp.int32, wide, 1)
    local = lax.broadcasted_iota(jnp.int32, wide, 0)

    def swap_vectors(xs, bit):
        step = 1 << bit
        split = [x.reshape(x.shape[0] // (2 * step), 2, step, 8, lanes) for x in xs]
        swap = split[0][:, 0] > split[0][:, 1]
        made = []
        for x in split:
            a, b = x[:, 0], x[:, 1]
            pair = [jnp.where(swap, b, a), jnp.where(swap, a, b)]
            made.append(jnp.stack(pair, axis=1).reshape(-1, 8, lanes))
        return made

    def swap_inside(xs, bit):
        if bit >= 3:
            step = 1 << (bit - 3)
            index = (lane_w ^ step).reshape(low * 8, lanes)
            upper = (lane_w & step) > 0
            others = [
                jnp.take_along_axis(x.reshape(low * 8, lanes), index, axis=1).reshape(wide)
                for x in xs
            ]
        else:
            step = 1 << bit
            upper = (sub_w & step) > 0
            others = []
            for x in xs:
                parts = []
                for u in range(low):
                    if step == 4:
                        parts.append(pltpu.roll(x[u], 4, axis=0))
                        continue
                    up, down = pltpu.roll(x[u], step, axis=0), pltpu.roll(x[u], 8 - step, axis=0)
                    parts.append(jnp.where((sub & step) > 0, up, down))
                others.append(jnp.stack(parts))
        key, other = xs[0], others[0]
        new = jnp.where(upper, jnp.maximum(key, other), jnp.minimum(key, other))
        take = new != key
        return [new] + [jnp.where(take, o, x) for x, o in zip(xs[1:], others[1:])]

    def flip(key, k, h):
        place = inside[None] + (h * low + local)
        bits = ((place >> (k - 1)) ^ (place >> k)) if k > 1 else (place >> 1)
        return key ^ -(bits & 1)

    def near(h, carry, k):
        xs = [ref[h] for ref in refs]
        if k is None:
            for m in range(1, low_bits + 1):
                xs[0] = flip(xs[0], m, h)
                for bit in reversed(range(m)):
                    xs = swap_vectors(xs, bit)
            nxt = low_bits + 1
        else:
            for bit in reversed(range(low_bits)):
                xs = swap_vectors(xs, bit)
            nxt = k + 1
        if nxt <= total_bits:
            xs[0] = flip(xs[0], nxt, h)
            for bit in reversed(range(vector_bits, nxt)):
                xs = swap_inside(xs, bit - vector_bits)
        for ref, x in zip(refs, xs):
            ref[h] = x
        return carry

    def far(l, carry, k):
        xs = [ref[:, l] for ref in refs]
        for bit in reversed(range(min(k, vector_bits) - low_bits)):
            xs = swap_vectors(xs, bit)
        for ref, x in zip(refs, xs):
            ref[:, l] = x
        return carry

    key_s[...] = keys[...].reshape(key_s.shape)
    for f, ref in enumerate(value_s):
        ref[...] = values[f].reshape(ref.shape)
    lax.fori_loop(0, high, lambda h, c: near(h, c, None), 0)
    for k in range(low_bits + 1, total_bits + 1):
        lax.fori_loop(0, low, lambda l, c, k=k: far(l, c, k), 0)
        lax.fori_loop(0, high, lambda h, c, k=k: near(h, c, k), 0)
    vectors = high * low
    per_lane = vectors * 8 // lanes
    used = out.shape[1] // per_lane
    for f, ref in enumerate(value_s):
        flat = ref.reshape(vectors * 8, lanes)
        rows_each = lanes // vectors
        for q in range(per_lane):
            parts = [flat[pl.ds(q * rows_each + s, vectors, stride=8), :] for s in range(rows_each)]
            turned = jnp.concatenate(parts, axis=0).T
            out[f, pl.ds(q, used, stride=per_lane), :] = turned[:used]

def order(slots_row, forces, count):
    rows = slots_row.shape[0] // lanes
    vectors = rows // 8
    shape = (vectors // 8, 8, 8, lanes)
    return pl.pallas_call(
        sort_kernel,
        out_shape=jax.ShapeDtypeStruct((3, count // lanes, lanes), F32),
        in_specs=[in_vmem, in_vmem],
        out_specs=in_vmem,
        scratch_shapes=[pltpu.VMEM(shape, jnp.int32)] + [pltpu.VMEM(shape, F32)] * 3,
        compiler_params=pltpu.CompilerParams(vmem_limit_bytes=vmem_limit),
    )(slots_row.reshape(rows, lanes), forces)
def on_device(
    positions,
    velocities,
    nodal_mass,
    thickness,
    pack_index,
    connectivity,
    tile_list,
    pair_mask,
    tile_count,
):
    both = ("wide", "narrow")
    owners = lax.axis_size("wide") * lax.axis_size("narrow")
    node_data = jnp.concatenate([positions, velocities, nodal_mass[None], thickness[None]], axis=0)
    slots_row = pack_index.reshape(-1)
    per_owner = slots_row.shape[0] // lanes // owners
    blocks = per_owner // 2
    halves = []
    for half in range(2):
        outgoing = pack(slots_row, node_data, owners, half * blocks, blocks)
        halves.append(
            lax.all_to_all(
                outgoing.reshape(owners, -1, 8, lanes), both, split_axis=0, concat_axis=0
            )
        )
    own_blocks = connectivity.shape[0] // seg_width
    edge = own_blocks // 4
    total, first_own, second_own, first_far, second_far = tile_pairs(
        tile_count, tile_list, own_blocks, own_blocks + 8 * edge
    )
    total, halves[1] = lax.optimization_barrier((total, halves[1]))
    edge_quads = edge * seg_width
    own_edge = segment_features(connectivity[:edge_quads], *halves)
    own_inner = segment_features(connectivity[edge_quads:], *halves)
    rim = with_neighbours(jnp.stack(with_neighbours(own_edge, "wide")), "narrow")
    slot_force = contact_pass(
        0, total[0:1], first_own, second_own, tile_list, *halves, pair_mask,
        [own_edge, own_inner], [(0, None), (1, None)], None,
    )
    around = [(b, a) for a in range(3) for b in range(3) if (a, b) != (1, 1)]
    slot_force = contact_pass(
        own_blocks, total[1:2], first_far, second_far, tile_list, *halves, pair_mask,
        list(rim), around, slot_force,
    )
    returned = lax.all_to_all(slot_force, both, split_axis=0, concat_axis=0)
    slot_forces = jnp.transpose(returned, (1, 0, 2, 3)).reshape(3, -1, lanes)
    return order(slots_row, slot_forces, positions.shape[1]).reshape(3, -1)


def solution(mesh):
    return jax.shard_map(
        on_device,
        mesh=mesh,
        in_specs=(
            P(None, ("wide", "narrow")),
            P(None, ("wide", "narrow")),
            P(("wide", "narrow")),
            P(("wide", "narrow")),
            P(("wide", "narrow"), None),
            P(("wide", "narrow"), None),
            P(None, ("wide", "narrow")),
            P(("wide", "narrow"), None),
            P(("wide", "narrow")),
        ),
        out_specs=P(None, ("wide", "narrow")),
        check_vma=False,
    )
```

time: 345 us -> 275 us (0.80)
  waiting for transfers between devices: 67.3 us -> 17 us
  Pallas kernels: 190 us -> 147 us
  blocking collectives: 48.1 us -> 73.5 us
  starting transfers between devices: 7.35 us -> 23.3 us
  between operations: 14.2 us -> 0.93 us
    all_to_all x1 -> x2, waiting for transfers between devices: 47.4 us -> 17 us  [on_device(): lax.all_to_all(outgoing.reshape(owners, -1, 8, lanes), both, split_axis=0...]
    all_to_all x1, blocking collectives: 48.1 us -> 73.5 us  [on_device(): returned = lax.all_to_all(slot_force, both, split_axis=0, concat_axis=0)]
    pallas_call x2, Pallas kernels: 52.9 us -> 30.9 us  [contact_pass(): pl.pallas_call(kernel, out_shape=jax.ShapeDtypeStruct((owners, 3, per_own...]
    all_gather x1 -> x0, waiting for transfers between devices: 19.9 us -> none  [on_device(): edges = lax.all_gather(own[:edge], both, axis=0, tiled=True)]
    pallas_call x2 -> x3, Pallas kernels: 109 us -> 92.3 us  [the longest x2 63.8 us: pack(): pl.pallas_call(partial(pack_kernel, first, blocks, per_owner), out_shape=...]
    ppermute x0 -> x4, starting transfers between devices: none -> 10.2 us  [the longest x2 7.58 us: with_neighbours(): before = lax.ppermute(cells, axis, [(i, i + 1) for i in range(ends)])]
    all_to_all x1 -> x2, starting transfers between devices: 7.31 us -> 13.1 us  [on_device(): lax.all_to_all(outgoing.reshape(owners, -1, 8, lanes), both, split_axis=0...]
    pallas_call x1, Pallas kernels: 10.5 us -> 6.66 us  [tile_pairs(): pl.pallas_call(partial(pair_kernel, own_blocks), out_shape=[jax.ShapeDtyp...]
  transfers between devices with their start and end apart: 2 -> 6, of which waited for: 2 -> 1; matrix products, arithmetic and copies ran while one was open for 1% -> 1% of each run, Pallas kernels for 9% -> 23%
where the time goes in v3:
time: 275 us; the launch traced here: 273 us
  Pallas kernels  147 us (53%)
  blocking collectives  73.5 us (27%)
  starting transfers between devices  23.3 us (8%)
  waiting for transfers between devices  17 us (6%)
  local copies, waits for them, and re-layouts  6.16 us (2%)
  other arithmetic  5.34 us (2%)
    all_to_all x1, blocking collectives, on_device(): returned = lax.all_to_all(slot_force, both, split_axis=0, concat_axis=0)  73.5 us
    pallas_call x2, Pallas kernels, pack(): pl.pallas_call(partial(pack_kernel, first, blocks, per_owner), out_shape=...  63.8 us
    pallas_call x2, Pallas kernels, contact_pass(): pl.pallas_call(kernel, out_shape=jax.ShapeDtypeStruct((owners, 3, per_own...  30.9 us
    pallas_call x1, Pallas kernels, order(): pl.pallas_call(sort_kernel, out_shape=jax.ShapeDtypeStruct((3, count // l...  28.5 us
    all_to_all x2, waiting for transfers between devices, on_device(): lax.all_to_all(outgoing.reshape(owners, -1, 8, lanes), both, split_axis=0...  17 us
    pallas_call x2, Pallas kernels, segment_features(): pl.pallas_call(feature_kernel, out_shape=jax.ShapeDtypeStruct((quads // s...  16.8 us
    all_to_all x2, starting transfers between devices, on_device(): lax.all_to_all(outgoing.reshape(owners, -1, 8, lanes), both, split_axis=0...  13.1 us
    ppermute x2, starting transfers between devices, with_neighbours(): before = lax.ppermute(cells, axis, [(i, i + 1) for i in range(ends)])  7.58 us
  transfers between devices with their start and end apart: 6, of which 1 were waited for; matrix products, arithmetic and copies ran while one was open for 1% of the time, Pallas kernels for 23%

profile of v3, /device:TPU:0, one launch (start us, length us, event | category | flops | bytes accessed | tf_op | source)
XLA Modules:
  0.0 272.9 jit_solution(4656050180429683545)
XLA Ops:
  0.0 3.5 %pad_maximum_fusion.nodes = f32[8,49152]{1,0:T(8,128)} fusion(f32[1,49152]{1,0:T(1,128)} %bitcast.71, f32[1,49152]{1,0:T(1,128)} %bitcast.72, f32[3,49152]{1,0:T(4,128)} %param.10, f32[3,49152]{1,0:T(4,128)} %param.9), kind=kLoop, calls=%fused_computation | loop fusion | flops 1179648 | bytes 3145728 | tf_op jit(solution)/shard_map/concatenate | solution.py:604
  3.5 31.9 %shard_map.93 = f32[256,8,128]{2,1,0:T(8,128)} custom-call(s32[65536]{0:T(1024)} %bitcast.67, f32[8,49152]{1,0:T(8,128)} %pad_maximum_fusion.nodes), custom_call_target="tpu_custom_call" | custom-call | tf_op jit(solution)/shard_map/pallas_call | solution.py:119
  35.4 7.3 %all-to-all-start.1 = ((f32[32,8,8,128]{3,2,1,0:T(8,128)}), f32[32,8,8,128]{3,2,1,0:T(8,128)S(1)}, u32[]{:S(2)}, u32[]{:S(2)}) async-start(f32[32,8,8,128]{3,2,1,0:T(8,128)} %bitcast.63), calls=%async_computation.1 | async-start | bytes 2097152 | tf_op jit(solution)/shard_map/all_to_all | solution.py:612
  42.7 31.9 %shard_map.91 = f32[256,8,128]{2,1,0:T(8,128)} custom-call(s32[65536]{0:T(1024)} %bitcast.68, f32[8,49152]{1,0:T(8,128)} %pad_maximum_fusion.nodes), custom_call_target="tpu_custom_call" | custom-call | tf_op jit(solution)/shard_map/pallas_call | solution.py:119
  74.6 0.0 slice-start
  74.6 0.0 all-to-all-done.1.half_b.refs_7_.refs_8_
  74.6 5.8 %all-to-all-start = ((f32[32,8,8,128]{3,2,1,0:T(8,128)}), f32[32,8,8,128]{3,2,1,0:T(8,128)S(1)}, u32[]{:S(2)}, u32[]{:S(2)}) async-start(f32[32,8,8,128]{3,2,1,0:T(8,128)} %bitcast.62), calls=%async_computation | async-start | bytes 2097152 | tf_op jit(solution)/shard_map/all_to_all | solution.py:612
  81.2 6.7 %shard_map.92 = (s32[2]{0:T(128)}, s32[640]{0:T(1024)}, s32[640]{0:T(1024)}, s32[640]{0:T(1024)}, s32[640]{0:T(1024)}) custom-call(s32[1]{0:T(128)S(6)} %copy.28.count_ref, s32[2,1024]{1,0:T(2,128)} %refs_6_.1), custom_call_target="tpu_custom_call" | custom-call | tf_op jit(solution)/shard_map/pallas_call | solution.py:306
  87.9 0.6 fusion.7
  88.5 0.6 add_select_fusion.2.place
  89.1 0.6 add_select_fusion.place
  89.7 17.0 %all-to-all-done.half_a.refs_6_.refs_7_ = f32[32,8,8,128]{3,2,1,0:T(8,128)S(1)} async-done(((f32[32,8,8,128]{3,2,1,0:T(8,128)}), f32[32,8,8,128]{3,2,1,0:T(8,128)S(1)}, u32[]{:S(2)}, u32[]{:S(2)}) %all-to-all-start) | async-done | bytes 1048608 | tf_op jit(solution)/shard_map/all_to_all | solution.py:612
  106.7 1.0 copy-done.1
  107.7 5.6 %shard_map.94.refs_0_ = f32[2,16,256]{2,1,0:T(8,128)} custom-call(s32[2048]{0:T(1024)} %bitcast.74, f32[32,8,8,128]{3,2,1,0:T(8,128)} %copy-done.1, f32[32,8,8,128]{3,2,1,0:T(8,128)} %copy-done, s32[4,4,128]{2,1,0:T(4,128)} %add_select_fusion.2.place), custom_call_target="tpu_custom_call" | custom-call | tf_op jit(solution)/shard_map/pallas_call | solution.py:217
  113.4 1.3 collective-permute-start.1
  114.7 4.5 %collective-permute-start = (f32[2,16,256]{2,1,0:T(8,128)}, f32[2,16,256]{2,1,0:T(8,128)S(1)}, u32[]{:S(2)}, u32[]{:S(2)}) collective-permute-start(f32[2,16,256]{2,1,0:T(8,128)} %shard_map.94.refs_0_), channel_id=1, source_target_pairs={{0,4},{4,8},{8,12},{12,16},{16,20},{20,24},{24,28},{1,5},{5,9},{9,... | collective-permute-start | bytes 98312 | tf_op jit(solution)/shard_map/ppermute | solution.py:471
  119.2 0.6 copy.17
  119.9 11.2 %shard_map.95.refs_1_ = f32[6,16,256]{2,1,0:T(8,128)} custom-call(s32[6144]{0:T(1024)} %bitcast.73, f32[32,8,8,128]{3,2,1,0:T(8,128)} %copy-done.1, f32[32,8,8,128]{3,2,1,0:T(8,128)} %copy-done, s32[4,12,128]{2,1,0:T(8,128)} %add_select_fusion.place), custom_call_target="tpu_custom_call" | custom-call | tf_op jit(solution)/shard_map/pallas_call | solution.py:217
  131.0 0.0 collective-permute-done.1
  131.0 0.0 collective-permute-done
  131.1 1.3 collective-permute-start.3
  132.4 3.0 %collective-permute-start.2 = (f32[3,2,16,256]{3,2,1,0:T(8,128)S(1)}, f32[3,2,16,256]{3,2,1,0:T(8,128)S(1)}, u32[]{:S(2)}, u32[]{:S(2)}) collective-permute-start(f32[3,2,16,256]{3,2,1,0:T(8,128)S(1)} %pad_maximum_fusion.1.refs_1_), channel_id=1, source_target_pairs={{0,1},{1,2},{2,3},{4,5},{5,6},{6,7},{8,9},{9,10},{10,11},{12,13},{... | collective-permute-start | bytes 294920 | tf_op jit(solution)/shard_map/ppermute | solution.py:471
  135.5 0.6 fusion.11
  136.0 12.9 %shard_map.96.refs_10_ = f32[32,3,16,128]{3,2,1,0:T(8,128)} custom-call(f32[2,16,256]{2,1,0:T(8,128)} %shard_map.94.refs_0_, f32[6,16,256]{2,1,0:T(8,128)} %shard_map.95.refs_1_, s32[1]{0:T(128)} %get-tuple-element.19.refs_2_, s32[640]{0:T(1024)} %get-tuple-element.17.refs_3_, s32[640]{0:T(1024)} %get-tuple-element.18.refs_4_, s32[2,1024]{1,0:T(2,128)} %refs_6_.1, ...), custom_call_target="tpu_custom_call" | custom-call | tf_op jit(solution)/shard_map/pallas_call | solution.py:452
  148.9 0.0 collective-permute-done.3.refs_2_
  149.0 0.6 copy-done.5
  149.6 0.0 copy-done.6
  149.6 18.0 %shard_map.97 = f32[32,3,16,128]{3,2,1,0:T(8,128)} custom-call(f32[3,2,16,256]{3,2,1,0:T(8,128)} %copy-done.6, f32[3,2,16,256]{3,2,1,0:T(8,128)} %copy-done.2, f32[3,2,16,256]{3,2,1,0:T(8,128)} %copy-done.5, s32[1]{0:T(128)} %get-tuple-element.20.refs_3_, s32[640]{0:T(1024)} %get-tuple-element.15.refs_4_, s32[640]{0:T(1024)} %get-tuple-element.16.refs_5_, ...), custom_call_target="tpu_custom_call" | custom-call | tf_op jit(solution)/shard_map/pallas_call | solution.py:452
  167.6 73.5 %all_to_all.15 = f32[32,3,16,128]{3,2,1,0:T(8,128)S(1)} all-to-all(f32[32,3,16,128]{3,2,1,0:T(8,128)} %shard_map.97), channel_id=1, replica_groups=mesh['wide'=8,'narrow'=4] {'wide','narrow'}, dimensions={0} | all-to-all | bytes 1572864 | tf_op jit(solution)/shard_map/all_to_all | solution.py:635
  241.1 0.9 copy.18
  242.0 28.5 %shard_map.98 = f32[3,384,128]{2,1,0:T(8,128)} custom-call(s32[512,128]{1,0:T(8,128)} %bitcast.69, f32[3,512,128]{2,1,0:T(8,128)} %bitcast.65), custom_call_target="tpu_custom_call" | custom-call | tf_op jit(solution)/shard_map/pallas_call | solution.py:583
  270.5 2.3 copy.27
  (20 shorter events, 0.1 us)
Async XLA Ops:
  35.4 39.3 %all-to-all-start.1 = ((f32[32,8,8,128]{3,2,1,0:T(8,128)}), f32[32,8,8,128]{3,2,1,0:T(8,128)S(1)}, u32[]{:S(2)}, u32[]{:S(2)}) async-start(f32[32,8,8,128]{3,2,1,0:T(8,128)} %bitcast.63), calls=%async_computation.1 | async-start | bytes 2097152 | tf_op jit(solution)/shard_map/all_to_all | solution.py:612
  74.6 6.5 %slice-start = ((s32[2048,4]{0,1:T(4,128)}), s32[1536,4]{0,1:T(4,128)S(1)}, s32[]{:S(2)}) async-start(s32[2048,4]{0,1:T(4,128)} %param.14), calls=%async_computation.3 | async-start | bytes 49152 | tf_op jit(solution)/shard_map/slice | solution.py:624
  74.6 13.2 %copy-start.4 = (s32[2048,4]{0,1:T(4,128)S(1)}, s32[2048,4]{0,1:T(4,128)}, u32[]{:S(2)}) copy-start(s32[2048,4]{0,1:T(4,128)} %param.14) | copy-start | bytes 98308
  74.6 32.1 %copy-start = (f32[32,8,8,128]{3,2,1,0:T(8,128)}, f32[32,8,8,128]{3,2,1,0:T(8,128)S(1)}, u32[]{:S(2)}) copy-start(f32[32,8,8,128]{3,2,1,0:T(8,128)S(1)} %all-to-all-done.1.half_b.refs_7_.refs_8_) | copy-start | bytes 3145732
  74.6 32.1 %all-to-all-start = ((f32[32,8,8,128]{3,2,1,0:T(8,128)}), f32[32,8,8,128]{3,2,1,0:T(8,128)S(1)}, u32[]{:S(2)}, u32[]{:S(2)}) async-start(f32[32,8,8,128]{3,2,1,0:T(8,128)} %bitcast.62), calls=%async_computation | async-start | bytes 2097152 | tf_op jit(solution)/shard_map/all_to_all | solution.py:612
  106.7 1.0 copy-start.1
  113.3 17.7 %copy-start.3 = (f32[2,16,256]{2,1,0:T(8,128)S(1)}, f32[2,16,256]{2,1,0:T(8,128)}, u32[]{:S(2)}) copy-start(f32[2,16,256]{2,1,0:T(8,128)} %shard_map.94.refs_0_) | copy-start | bytes 98308
  113.3 22.1 %copy-start.7 = (s32[2]{0:T(128)S(1)}, s32[2]{0:T(128)}, u32[]{:S(2)}) copy-start(s32[2]{0:T(128)} %get-tuple-element.14) | copy-start | bytes 28
  113.4 17.7 %collective-permute-start.1 = (f32[2,16,256]{2,1,0:T(8,128)}, f32[2,16,256]{2,1,0:T(8,128)S(1)}, u32[]{:S(2)}, u32[]{:S(2)}) collective-permute-start(f32[2,16,256]{2,1,0:T(8,128)} %shard_map.94.refs_0_), channel_id=1, source_target_pairs={{4,0},{8,4},{12,8},{16,12},{20,16},{24,20},{28,24},{5,1},{9,5},{13... | collective-permute-start | bytes 98312 | tf_op jit(solution)/shard_map/ppermute | solution.py:472
  114.7 16.4 %collective-permute-start = (f32[2,16,256]{2,1,0:T(8,128)}, f32[2,16,256]{2,1,0:T(8,128)S(1)}, u32[]{:S(2)}, u32[]{:S(2)}) collective-permute-start(f32[2,16,256]{2,1,0:T(8,128)} %shard_map.94.refs_0_), channel_id=1, source_target_pairs={{0,4},{4,8},{8,12},{12,16},{16,20},{20,24},{24,28},{1,5},{5,9},{9,... | collective-permute-start | bytes 98312 | tf_op jit(solution)/shard_map/ppermute | solution.py:471
  131.1 17.8 %copy-start.2 = (f32[3,2,16,256]{3,2,1,0:T(8,128)}, f32[3,2,16,256]{3,2,1,0:T(8,128)S(1)}, u32[]{:S(2)}) copy-start(f32[3,2,16,256]{3,2,1,0:T(8,128)S(1)} %pad_maximum_fusion.1.refs_1_) | copy-start | bytes 294916
  131.1 17.8 %collective-permute-start.3 = (f32[3,2,16,256]{3,2,1,0:T(8,128)S(1)}, f32[3,2,16,256]{3,2,1,0:T(8,128)S(1)}, u32[]{:S(2)}, u32[]{:S(2)}) collective-permute-start(f32[3,2,16,256]{3,2,1,0:T(8,128)S(1)} %pad_maximum_fusion.1.refs_1_), channel_id=1, source_target_pairs={{1,0},{2,1},{3,2},{5,4},{6,5},{7,6},{9,8},{10,9},{11,10},{13,12},{... | collective-permute-start | bytes 294920 | tf_op jit(solution)/shard_map/ppermute | solution.py:472
  132.4 16.6 %collective-permute-start.2 = (f32[3,2,16,256]{3,2,1,0:T(8,128)S(1)}, f32[3,2,16,256]{3,2,1,0:T(8,128)S(1)}, u32[]{:S(2)}, u32[]{:S(2)}) collective-permute-start(f32[3,2,16,256]{3,2,1,0:T(8,128)S(1)} %pad_maximum_fusion.1.refs_1_), channel_id=1, source_target_pairs={{0,1},{1,2},{2,3},{4,5},{5,6},{6,7},{8,9},{9,10},{10,11},{12,13},{... | collective-permute-start | bytes 294920 | tf_op jit(solution)/shard_map/ppermute | solution.py:471
  148.9 0.6 copy-start.5
  149.0 0.7 copy-start.6

commit v4 on v3

--- a/solution.py
+++ b/solution.py
@@ -13,7 +13,7 @@
 lanes = 128
 groups = 16
 span = lanes * groups
-half_span = span // 2
+index_parts = 4
 seg_width = 256
 table_unroll = 4
 pairs_per_turn = 16
@@ -27,20 +27,22 @@
 
 
 def pack_kernel(
-    first, blocks, per_owner, index_ref, nodes, out, table, rows, parts, buffer_a, buffer_b, sems
+    first, blocks, per_owner, index_ref, place, speed, mass, height,
+    out, table, rows, parts, *buffers_and_sems,
 ):
-    count = nodes.shape[1]
+    count = place.shape[1]
     supers = count // span
-    buffers = (buffer_a, buffer_b)
+    *buffers, sems = buffers_and_sems
     turns = out.shape[0] // groups
-    piece = math.gcd(blocks * lanes, half_span)
-    pieces = half_span // piece
+    part_slots = span // index_parts
+    piece = math.gcd(blocks * lanes, part_slots)
+    pieces = part_slots // piece
     owner_pieces = blocks * lanes // piece
 
     def fetch(turn, part):
         copies = []
         for k in range(pieces):
-            number = (turn * 2 + part) * pieces + k
+            number = (turn * index_parts + part) * pieces + k
             start = (number // owner_pieces * per_owner + first) * lanes
             start = start + number % owner_pieces * piece
             copies.append(
@@ -52,16 +54,22 @@
             )
         return copies
 
-    for part in range(2):
+    for part in range(index_parts):
         for copy in fetch(0, part):
             copy.start()
 
     def turn_around(step, carry):
         for i in range(table_unroll):
             number = step * table_unroll + i
-            states = nodes[:, pl.ds(pl.multiple_of(number * span, span), span)]
+            here = pl.ds(pl.multiple_of(number * span, span), span)
+            states = [ref[:, here] for ref in (place, speed, mass, height)]
             stacked = jnp.concatenate(
-                [states[:, g * lanes : (g + 1) * lanes] for g in range(groups)], axis=0
+                [
+                    state[:, g * lanes : (g + 1) * lanes]
+                    for g in range(groups)
+                    for state in states
+                ],
+                axis=0,
             )
             at = pl.ds(pl.multiple_of(number * lanes, lanes), lanes)
             for k, part in enumerate(three_parts(stacked.T)):
@@ -93,12 +101,13 @@
     table[count : count + 8, :] = jnp.zeros((8, lanes), F32)
 
     def body(turn, carry):
-        for part in range(2):
+        for part in range(index_parts):
             for copy in fetch(turn, part):
                 copy.wait()
             for j in range(lanes):
-                for i in range(groups // 2):
-                    cols = slice((part * groups // 2 + i) * 8, (part * groups // 2 + i + 1) * 8)
+                for i in range(groups // index_parts):
+                    g = part * groups // index_parts + i
+                    cols = slice(g * 8, g * 8 + 8)
                     row = buffers[part][i * lanes + j]
                     rows[j : j + 1, cols] = table[pl.ds(row, 1), cols]
 
@@ -113,24 +122,24 @@
     lax.fori_loop(0, turns, body, 0)
 
 
-def pack(slots_row, node_data, owners, first, blocks):
+def pack(slots_row, node_arrays, owners, first, blocks):
     per_owner = slots_row.shape[0] // lanes // owners
-    count = node_data.shape[1]
+    count = node_arrays[0].shape[1]
+    part_slots = span // index_parts
     return pl.pallas_call(
         partial(pack_kernel, first, blocks, per_owner),
         out_shape=jax.ShapeDtypeStruct((owners * blocks, 8, lanes), F32),
-        in_specs=[in_hbm, in_vmem],
+        in_specs=[in_hbm] + [in_vmem] * 4,
         out_specs=in_vmem,
         scratch_shapes=[
             pltpu.VMEM((count + 8, lanes), F32),
             pltpu.VMEM((lanes, lanes), F32),
             pltpu.VMEM((count // groups, 3 * lanes), BF16),
-            pltpu.SMEM((half_span,), jnp.int32),
-            pltpu.SMEM((half_span,), jnp.int32),
-            pltpu.SemaphoreType.DMA((2, half_span // math.gcd(blocks * lanes, half_span))),
+            *[pltpu.SMEM((part_slots,), jnp.int32)] * index_parts,
+            pltpu.SemaphoreType.DMA((index_parts, part_slots // math.gcd(blocks * lanes, part_slots))),
         ],
         compiler_params=pltpu.CompilerParams(vmem_limit_bytes=vmem_limit),
-    )(slots_row, node_data)
+    )(slots_row, *node_arrays)
 
 
 def quad_features(corners):
@@ -314,9 +323,17 @@
 
 def contact_kernel(
     first_block, plan, part_refs, total_ref, firsts, seconds, list_ref,
-    half_a, half_b, mask, before, out, features, seg_side, normals, masked, nodes, half_sems,
+    half_a, half_b, mask_hbm, before, out, features, seg_side, normals, masked, nodes,
+    mask, half_sems,
 ):
-    node_copies = load_halves((half_a, half_b), nodes, half_sems)
+    copies = load_halves((half_a, half_b), nodes, half_sems)
+    copies.append(pltpu.make_async_copy(mask_hbm, mask, half_sems.at[2]))
+    copies[-1].start()
+    if before is None:
+        out[...] = jnp.zeros(out.shape, F32)
+    else:
+        copies.append(pltpu.make_async_copy(before, out, half_sems.at[3]))
+        copies[-1].start()
     filled = 0
     for which, at in plan:
         part = part_refs[which] if at is None else part_refs[which].at[at]
@@ -351,13 +368,9 @@
 
     together = math.gcd(features.shape[0], 4)
     lax.fori_loop(0, features.shape[0] // together, prepare_some, 0)
-    if before is None:
-        out[...] = jnp.zeros(out.shape, F32)
-    else:
-        out[...] = before[...]
     masked[...] = jnp.zeros(masked.shape, F32)
     per_owner = out.shape[2]
-    for copy in node_copies:
+    for copy in copies:
         copy.wait()
     row = lax.broadcasted_iota(jnp.int32, (8, lanes), 0)
     mask_row = lax.broadcasted_iota(jnp.int32, (32, 2 * lanes), 0)
@@ -445,10 +458,10 @@
         contact_kernel(first_block, plan, part_refs, *rest)
 
     operands = [*parts, total, firsts, seconds, tile_list, half_a, half_b, pair_mask]
-    specs = [in_vmem] * len(parts) + [in_smem] * 4 + [in_hbm] * 2 + [in_vmem]
+    specs = [in_vmem] * len(parts) + [in_smem] * 4 + [in_hbm] * 3
     if not first_call:
         operands.append(before)
-        specs.append(in_vmem)
+        specs.append(in_hbm)
     return pl.pallas_call(
         kernel,
         out_shape=jax.ShapeDtypeStruct((owners, 3, per_owner, lanes), F32),
@@ -460,7 +473,8 @@
             pltpu.VMEM((seg_blocks, 3, seg_width, lanes), F32),
             pltpu.VMEM((lanes, seg_width), F32),
             pltpu.VMEM((owners, per_owner, 8, lanes), F32),
-            pltpu.SemaphoreType.DMA((2,)),
+            pltpu.VMEM(pair_mask.shape, jnp.int32),
+            pltpu.SemaphoreType.DMA((4,)),
         ],
         compiler_params=pltpu.CompilerParams(vmem_limit_bytes=vmem_limit),
     )(*operands)
@@ -482,7 +496,8 @@
     lane = lax.broadcasted_iota(jnp.int32, (8, lanes), 1)
     sub = lax.broadcasted_iota(jnp.int32, (8, lanes), 0)
     inside = (lane * 8 + sub) << vector_bits
-    wide = (low, 8, lanes)
+    runs = math.gcd(high, 2)
+    wide = (runs * low, 8, lanes)
     lane_w = lax.broadcasted_iota(jnp.int32, wide, 2)
     sub_w = lax.broadcasted_iota(jnp.int32, wide, 1)
     local = lax.broadcasted_iota(jnp.int32, wide, 0)
@@ -501,10 +516,10 @@
     def swap_inside(xs, bit):
         if bit >= 3:
             step = 1 << (bit - 3)
-            index = (lane_w ^ step).reshape(low * 8, lanes)
+            index = (lane_w ^ step).reshape(-1, lanes)
             upper = (lane_w & step) > 0
             others = [
-                jnp.take_along_axis(x.reshape(low * 8, lanes), index, axis=1).reshape(wide)
+                jnp.take_along_axis(x.reshape(-1, lanes), index, axis=1).reshape(wide)
                 for x in xs
             ]
         else:
@@ -513,7 +528,7 @@
             others = []
             for x in xs:
                 parts = []
-                for u in range(low):
+                for u in range(runs * low):
                     if step == 4:
                         parts.append(pltpu.roll(x[u], 4, axis=0))
                         continue
@@ -526,12 +541,12 @@
         return [new] + [jnp.where(take, o, x) for x, o in zip(xs[1:], others[1:])]
 
     def flip(key, k, h):
-        place = inside[None] + (h * low + local)
+        place = inside[None] + (h * runs * low + local)
         bits = ((place >> (k - 1)) ^ (place >> k)) if k > 1 else (place >> 1)
         return key ^ -(bits & 1)
 
     def near(h, carry, k):
-        xs = [ref[h] for ref in refs]
+        xs = [ref[pl.ds(h * runs, runs)].reshape(wide) for ref in refs]
         if k is None:
             for m in range(1, low_bits + 1):
                 xs[0] = flip(xs[0], m, h)
@@ -547,7 +562,7 @@
             for bit in reversed(range(vector_bits, nxt)):
                 xs = swap_inside(xs, bit - vector_bits)
         for ref, x in zip(refs, xs):
-            ref[h] = x
+            ref[pl.ds(h * runs, runs)] = x.reshape(runs, low, 8, lanes)
         return carry
 
     def far(l, carry, k):
@@ -560,11 +575,11 @@
 
     key_s[...] = keys[...].reshape(key_s.shape)
     for f, ref in enumerate(value_s):
-        ref[...] = values[f].reshape(ref.shape)
-    lax.fori_loop(0, high, lambda h, c: near(h, c, None), 0)
+        ref[...] = values[:, f].reshape(ref.shape)
+    lax.fori_loop(0, high // runs, lambda h, c: near(h, c, None), 0)
     for k in range(low_bits + 1, total_bits + 1):
         lax.fori_loop(0, low, lambda l, c, k=k: far(l, c, k), 0)
-        lax.fori_loop(0, high, lambda h, c, k=k: near(h, c, k), 0)
+        lax.fori_loop(0, high // runs, lambda h, c, k=k: near(h, c, k), 0)
     vectors = high * low
     per_lane = vectors * 8 // lanes
     used = out.shape[1] // per_lane
@@ -575,6 +590,7 @@
             parts = [flat[pl.ds(q * rows_each + s, vectors, stride=8), :] for s in range(rows_each)]
             turned = jnp.concatenate(parts, axis=0).T
             out[f, pl.ds(q, used, stride=per_lane), :] = turned[:used]
+
 
 def order(slots_row, forces, count):
     rows = slots_row.shape[0] // lanes
@@ -588,6 +604,8 @@
         scratch_shapes=[pltpu.VMEM(shape, jnp.int32)] + [pltpu.VMEM(shape, F32)] * 3,
         compiler_params=pltpu.CompilerParams(vmem_limit_bytes=vmem_limit),
     )(slots_row.reshape(rows, lanes), forces)
+
+
 def on_device(
     positions,
     velocities,
@@ -601,13 +619,13 @@
 ):
     both = ("wide", "narrow")
     owners = lax.axis_size("wide") * lax.axis_size("narrow")
-    node_data = jnp.concatenate([positions, velocities, nodal_mass[None], thickness[None]], axis=0)
+    node_arrays = (positions, velocities, nodal_mass[None], thickness[None])
     slots_row = pack_index.reshape(-1)
     per_owner = slots_row.shape[0] // lanes // owners
     blocks = per_owner // 2
     halves = []
     for half in range(2):
-        outgoing = pack(slots_row, node_data, owners, half * blocks, blocks)
+        outgoing = pack(slots_row, node_arrays, owners, half * blocks, blocks)
         halves.append(
             lax.all_to_all(
                 outgoing.reshape(owners, -1, 8, lanes), both, split_axis=0, concat_axis=0
@@ -633,8 +651,9 @@
         list(rim), around, slot_force,
     )
     returned = lax.all_to_all(slot_force, both, split_axis=0, concat_axis=0)
-    slot_forces = jnp.transpose(returned, (1, 0, 2, 3)).reshape(3, -1, lanes)
-    return order(slots_row, slot_forces, positions.shape[1]).reshape(3, -1)
+    if per_owner % 8:
+        returned = jnp.transpose(returned, (1, 0, 2, 3)).reshape(1, 3, -1, lanes)
+    return order(slots_row, returned, positions.shape[1]).reshape(3, -1)
 
 
 def solution(mesh):

time: 275 us -> 261 us (0.949)
  Pallas kernels: 147 us -> 135 us
  other arithmetic: 5.34 us -> 1.88 us
    pallas_call x1, Pallas kernels: 28.5 us -> 21.1 us  [order(): pl.pallas_call(sort_kernel, out_shape=jax.ShapeDtypeStruct((3, count // l...]
    concatenate x1 -> x0, other arithmetic: 3.46 us -> none  [on_device(): jnp.concatenate([positions, velocities, nodal_mass[None], thickness[None]...]
where the time goes in v4:
time: 261 us; the launch traced here: 259 us
  Pallas kernels  135 us (52%)
  blocking collectives  74.4 us (29%)
  starting transfers between devices  23.3 us (9%)
  waiting for transfers between devices  16.8 us (6%)
  local copies, waits for them, and re-layouts  6.91 us (3%)
    all_to_all x1, blocking collectives, on_device(): returned = lax.all_to_all(slot_force, both, split_axis=0, concat_axis=0)  74.4 us
    pallas_call x2, Pallas kernels, pack(): pl.pallas_call(partial(pack_kernel, first, blocks, per_owner), out_shape=...  62.8 us
    pallas_call x2, Pallas kernels, contact_pass(): pl.pallas_call(kernel, out_shape=jax.ShapeDtypeStruct((owners, 3, per_own...  28.2 us
    pallas_call x1, Pallas kernels, order(): pl.pallas_call(sort_kernel, out_shape=jax.ShapeDtypeStruct((3, count // l...  21.1 us
    pallas_call x2, Pallas kernels, segment_features(): pl.pallas_call(feature_kernel, out_shape=jax.ShapeDtypeStruct((quads // s...  16.8 us
    all_to_all x2, waiting for transfers between devices, on_device(): lax.all_to_all(outgoing.reshape(owners, -1, 8, lanes), both, split_axis=0...  16.8 us
    all_to_all x2, starting transfers between devices, on_device(): lax.all_to_all(outgoing.reshape(owners, -1, 8, lanes), both, split_axis=0...  13.1 us
    ppermute x2, starting transfers between devices, with_neighbours(): before = lax.ppermute(cells, axis, [(i, i + 1) for i in range(ends)])  7.58 us
  transfers between devices with their start and end apart: 6, of which 1 were waited for; matrix products, arithmetic and copies ran while one was open for 1% of the time, Pallas kernels for 23%

profile of v4, /device:TPU:0, one launch (start us, length us, event | category | flops | bytes accessed | tf_op | source)
XLA Modules:
  0.0 259.3 jit_solution(9709685785202523286)
XLA Ops:
  0.0 31.4 %shard_map.93 = f32[256,8,128]{2,1,0:T(8,128)} custom-call(s32[65536]{0:T(1024)} %bitcast.62, f32[3,49152]{1,0:T(4,128)} %place.3, f32[3,49152]{1,0:T(4,128)} %speed.3, f32[1,49152]{1,0:T(1,128)} %bitcast.66, f32[1,49152]{1,0:T(1,128)} %bitcast.68), custom_call_target="tpu_custom_call" | custom-call | tf_op jit(solution)/shard_map/pallas_call | solution.py:129
  31.4 7.3 %all-to-all-start.1 = ((f32[32,8,8,128]{3,2,1,0:T(8,128)}), f32[32,8,8,128]{3,2,1,0:T(8,128)S(1)}, u32[]{:S(2)}, u32[]{:S(2)}) async-start(f32[32,8,8,128]{3,2,1,0:T(8,128)} %bitcast.61), calls=%async_computation.1 | async-start | bytes 2097152 | tf_op jit(solution)/shard_map/all_to_all | solution.py:630
  38.7 31.4 %shard_map.91 = f32[256,8,128]{2,1,0:T(8,128)} custom-call(s32[65536]{0:T(1024)} %bitcast.63, f32[3,49152]{1,0:T(4,128)} %place.3, f32[3,49152]{1,0:T(4,128)} %speed.3, f32[1,49152]{1,0:T(1,128)} %bitcast.67, f32[1,49152]{1,0:T(1,128)} %bitcast.69), custom_call_target="tpu_custom_call" | custom-call | tf_op jit(solution)/shard_map/pallas_call | solution.py:129
  70.1 0.0 all-to-all-done.1.half_b.refs_7_.refs_8_
  70.2 1.0 copy-done
  71.1 5.8 %all-to-all-start = ((f32[32,8,8,128]{3,2,1,0:T(8,128)}), f32[32,8,8,128]{3,2,1,0:T(8,128)S(1)}, u32[]{:S(2)}, u32[]{:S(2)}) async-start(f32[32,8,8,128]{3,2,1,0:T(8,128)} %bitcast.60), calls=%async_computation | async-start | bytes 2097152 | tf_op jit(solution)/shard_map/all_to_all | solution.py:630
  77.6 0.0 slice-start
  77.6 0.7 slice-done
  78.4 6.2 %shard_map.92 = (s32[2]{0:T(128)}, s32[640]{0:T(1024)}, s32[640]{0:T(1024)}, s32[640]{0:T(1024)}, s32[640]{0:T(1024)}) custom-call(s32[1]{0:T(128)S(6)} %copy.26.count_ref, s32[2,1024]{1,0:T(2,128)} %refs_6_.1), custom_call_target="tpu_custom_call" | custom-call | tf_op jit(solution)/shard_map/pallas_call | solution.py:315
  84.6 0.6 fusion.7
  85.2 0.6 add_select_fusion.2.place
  85.8 0.6 add_select_fusion.place
  86.4 16.8 %all-to-all-done.half_a.refs_6_.refs_7_ = f32[32,8,8,128]{3,2,1,0:T(8,128)S(1)} async-done(((f32[32,8,8,128]{3,2,1,0:T(8,128)}), f32[32,8,8,128]{3,2,1,0:T(8,128)S(1)}, u32[]{:S(2)}, u32[]{:S(2)}) %all-to-all-start) | async-done | bytes 1048608 | tf_op jit(solution)/shard_map/all_to_all | solution.py:630
  103.2 1.0 copy-done.1
  104.2 5.6 %shard_map.94.refs_0_ = f32[2,16,256]{2,1,0:T(8,128)} custom-call(s32[2048]{0:T(1024)} %bitcast.72, f32[32,8,8,128]{3,2,1,0:T(8,128)} %copy-done.1, f32[32,8,8,128]{3,2,1,0:T(8,128)} %copy-done, s32[4,4,128]{2,1,0:T(4,128)} %add_select_fusion.2.place), custom_call_target="tpu_custom_call" | custom-call | tf_op jit(solution)/shard_map/pallas_call | solution.py:226
  109.8 1.3 collective-permute-start.1
  111.1 4.5 %collective-permute-start = (f32[2,16,256]{2,1,0:T(8,128)}, f32[2,16,256]{2,1,0:T(8,128)S(1)}, u32[]{:S(2)}, u32[]{:S(2)}) collective-permute-start(f32[2,16,256]{2,1,0:T(8,128)} %shard_map.94.refs_0_), channel_id=1, source_target_pairs={{0,4},{4,8},{8,12},{12,16},{16,20},{20,24},{24,28},{1,5},{5,9},{9,... | collective-permute-start | bytes 98312 | tf_op jit(solution)/shard_map/ppermute | solution.py:485
  115.7 0.6 copy.16
  116.3 11.2 %shard_map.95.refs_1_ = f32[6,16,256]{2,1,0:T(8,128)} custom-call(s32[6144]{0:T(1024)} %bitcast.71, f32[32,8,8,128]{3,2,1,0:T(8,128)} %copy-done.1, f32[32,8,8,128]{3,2,1,0:T(8,128)} %copy-done, s32[4,12,128]{2,1,0:T(8,128)} %add_select_fusion.place), custom_call_target="tpu_custom_call" | custom-call | tf_op jit(solution)/shard_map/pallas_call | solution.py:226
  127.5 0.0 collective-permute-done
  127.6 1.3 collective-permute-start.3
  128.9 3.0 %collective-permute-start.2 = (f32[3,2,16,256]{3,2,1,0:T(8,128)S(1)}, f32[3,2,16,256]{3,2,1,0:T(8,128)S(1)}, u32[]{:S(2)}, u32[]{:S(2)}) collective-permute-start(f32[3,2,16,256]{3,2,1,0:T(8,128)S(1)} %pad_maximum_fusion.refs_1_), channel_id=1, source_target_pairs={{0,1},{1,2},{2,3},{4,5},{5,6},{6,7},{8,9},{9,10},{10,11},{12,13},{... | collective-permute-start | bytes 294920 | tf_op jit(solution)/shard_map/ppermute | solution.py:485
  131.9 0.6 fusion.11
  132.5 10.8 %shard_map.96.refs_10_ = f32[32,3,16,128]{3,2,1,0:T(8,128)} custom-call(f32[2,16,256]{2,1,0:T(8,128)} %shard_map.94.refs_0_, f32[6,16,256]{2,1,0:T(8,128)} %shard_map.95.refs_1_, s32[1]{0:T(128)} %get-tuple-element.19.refs_2_, s32[640]{0:T(1024)} %get-tuple-element.17.refs_3_, s32[640]{0:T(1024)} %get-tuple-element.18.refs_4_, s32[2,1024]{1,0:T(2,128)} %refs_6_.1, ...), custom_call_target="tpu_custom_call" | custom-call | tf_op jit(solution)/shard_map/pallas_call | solution.py:465
  143.3 0.0 collective-permute-done.3.refs_2_
  143.3 0.0 collective-permute-done.2.refs_0_
  143.4 0.6 copy-done.5
  144.0 0.0 copy-done.6
  144.0 17.4 %shard_map.97 = f32[32,3,16,128]{3,2,1,0:T(8,128)} custom-call(f32[3,2,16,256]{3,2,1,0:T(8,128)} %copy-done.6, f32[3,2,16,256]{3,2,1,0:T(8,128)} %copy-done.2, f32[3,2,16,256]{3,2,1,0:T(8,128)} %copy-done.5, s32[1]{0:T(128)} %get-tuple-element.20.refs_3_, s32[640]{0:T(1024)} %get-tuple-element.15.refs_4_, s32[640]{0:T(1024)} %get-tuple-element.16.refs_5_, ...), custom_call_target="tpu_custom_call" | custom-call | tf_op jit(solution)/shard_map/pallas_call | solution.py:465
  161.4 74.4 %all_to_all.15.values = f32[32,3,16,128]{3,2,1,0:T(8,128)} all-to-all(f32[32,3,16,128]{3,2,1,0:T(8,128)} %shard_map.97), channel_id=1, replica_groups=mesh['wide'=8,'narrow'=4] {'wide','narrow'}, dimensions={0} | all-to-all | bytes 1572864 | tf_op jit(solution)/shard_map/all_to_all | solution.py:653
  235.8 21.1 %shard_map.98 = f32[3,384,128]{2,1,0:T(8,128)} custom-call(s32[512,128]{1,0:T(8,128)} %bitcast.64, f32[32,3,16,128]{3,2,1,0:T(8,128)} %all_to_all.15.values), custom_call_target="tpu_custom_call" | custom-call | tf_op jit(solution)/shard_map/pallas_call | solution.py:599
  256.9 2.3 copy.25
  (18 shorter events, 0.1 us)
Async XLA Ops:
  31.4 38.7 %all-to-all-start.1 = ((f32[32,8,8,128]{3,2,1,0:T(8,128)}), f32[32,8,8,128]{3,2,1,0:T(8,128)S(1)}, u32[]{:S(2)}, u32[]{:S(2)}) async-start(f32[32,8,8,128]{3,2,1,0:T(8,128)} %bitcast.61), calls=%async_computation.1 | async-start | bytes 2097152 | tf_op jit(solution)/shard_map/all_to_all | solution.py:630
  70.2 1.0 copy-start
  71.1 32.1 %all-to-all-start = ((f32[32,8,8,128]{3,2,1,0:T(8,128)}), f32[32,8,8,128]{3,2,1,0:T(8,128)S(1)}, u32[]{:S(2)}, u32[]{:S(2)}) async-start(f32[32,8,8,128]{3,2,1,0:T(8,128)} %bitcast.60), calls=%async_computation | async-start | bytes 2097152 | tf_op jit(solution)/shard_map/all_to_all | solution.py:630
  77.6 0.7 slice-start
  78.4 6.2 %copy-start.4 = (s32[2048,4]{0,1:T(4,128)S(1)}, s32[2048,4]{0,1:T(4,128)}, u32[]{:S(2)}) copy-start(s32[2048,4]{0,1:T(4,128)} %param.14) | copy-start | bytes 98308
  103.2 1.0 copy-start.1
  109.8 17.7 %collective-permute-start.1 = (f32[2,16,256]{2,1,0:T(8,128)}, f32[2,16,256]{2,1,0:T(8,128)S(1)}, u32[]{:S(2)}, u32[]{:S(2)}) collective-permute-start(f32[2,16,256]{2,1,0:T(8,128)} %shard_map.94.refs_0_), channel_id=1, source_target_pairs={{4,0},{8,4},{12,8},{16,12},{20,16},{24,20},{28,24},{5,1},{9,5},{13... | collective-permute-start | bytes 98312 | tf_op jit(solution)/shard_map/ppermute | solution.py:486
  111.1 16.4 %collective-permute-start = (f32[2,16,256]{2,1,0:T(8,128)}, f32[2,16,256]{2,1,0:T(8,128)S(1)}, u32[]{:S(2)}, u32[]{:S(2)}) collective-permute-start(f32[2,16,256]{2,1,0:T(8,128)} %shard_map.94.refs_0_), channel_id=1, source_target_pairs={{0,4},{4,8},{8,12},{12,16},{16,20},{20,24},{24,28},{1,5},{5,9},{9,... | collective-permute-start | bytes 98312 | tf_op jit(solution)/shard_map/ppermute | solution.py:485
  116.3 11.2 %copy-start.3 = (f32[2,16,256]{2,1,0:T(8,128)S(1)}, f32[2,16,256]{2,1,0:T(8,128)}, u32[]{:S(2)}) copy-start(f32[2,16,256]{2,1,0:T(8,128)} %shard_map.94.refs_0_) | copy-start | bytes 98308
  127.5 4.4 %copy-start.7 = (s32[2]{0:T(128)S(1)}, s32[2]{0:T(128)}, u32[]{:S(2)}) copy-start(s32[2]{0:T(128)} %get-tuple-element.14) | copy-start | bytes 28
  127.6 15.7 %copy-start.2 = (f32[3,2,16,256]{3,2,1,0:T(8,128)}, f32[3,2,16,256]{3,2,1,0:T(8,128)S(1)}, u32[]{:S(2)}) copy-start(f32[3,2,16,256]{3,2,1,0:T(8,128)S(1)} %pad_maximum_fusion.refs_1_) | copy-start | bytes 294916
  127.6 15.7 %collective-permute-start.3 = (f32[3,2,16,256]{3,2,1,0:T(8,128)S(1)}, f32[3,2,16,256]{3,2,1,0:T(8,128)S(1)}, u32[]{:S(2)}, u32[]{:S(2)}) collective-permute-start(f32[3,2,16,256]{3,2,1,0:T(8,128)S(1)} %pad_maximum_fusion.refs_1_), channel_id=1, source_target_pairs={{1,0},{2,1},{3,2},{5,4},{6,5},{7,6},{9,8},{10,9},{11,10},{13,12},{... | collective-permute-start | bytes 294920 | tf_op jit(solution)/shard_map/ppermute | solution.py:486
  128.9 14.5 %collective-permute-start.2 = (f32[3,2,16,256]{3,2,1,0:T(8,128)S(1)}, f32[3,2,16,256]{3,2,1,0:T(8,128)S(1)}, u32[]{:S(2)}, u32[]{:S(2)}) collective-permute-start(f32[3,2,16,256]{3,2,1,0:T(8,128)S(1)} %pad_maximum_fusion.refs_1_), channel_id=1, source_target_pairs={{0,1},{1,2},{2,3},{4,5},{5,6},{6,7},{8,9},{9,10},{10,11},{12,13},{... | collective-permute-start | bytes 294920 | tf_op jit(solution)/shard_map/ppermute | solution.py:485
  143.3 0.6 copy-start.5
  143.3 0.7 copy-start.6

commit v5 on v4

--- a/solution.py
+++ b/solution.py
@@ -27,12 +27,26 @@
 
 
 def pack_kernel(
-    first, blocks, per_owner, index_ref, place, speed, mass, height,
-    out, table, rows, parts, *buffers_and_sems,
+    first, blocks, per_owner, index_ref, place_hbm, speed_hbm, mass_hbm, height_hbm, out,
+    place, speed, mass, height, stage, table, rows, parts, *buffers_and_sems,
 ):
     count = place.shape[1]
     supers = count // span
-    *buffers, sems = buffers_and_sems
+    *buffers, sems, in_sems, out_sems = buffers_and_sems
+    sources = (place_hbm, speed_hbm, mass_hbm, height_hbm)
+
+    def bring(step):
+        at = pl.ds(pl.multiple_of(step * table_unroll * span, span), table_unroll * span)
+        return [
+            pltpu.make_async_copy(source.at[:, at], target.at[:, at], in_sems.at[step, k])
+            for k, (source, target) in enumerate(zip(sources, (place, speed, mass, height)))
+        ]
+
+    def send(turn):
+        slot = turn % 2
+        to = out.at[pl.ds(turn * groups, groups)]
+        return pltpu.make_async_copy(stage.at[slot], to, out_sems.at[slot])
+
     turns = out.shape[0] // groups
     part_slots = span // index_parts
     piece = math.gcd(blocks * lanes, part_slots)
@@ -58,7 +72,13 @@
         for copy in fetch(0, part):
             copy.start()
 
+    for step in range(supers // table_unroll):
+        for copy in bring(step):
+            copy.start()
+
     def turn_around(step, carry):
+        for copy in bring(step):
+            copy.wait()
         for i in range(table_unroll):
             number = step * table_unroll + i
             here = pl.ds(pl.multiple_of(number * span, span), span)
@@ -116,10 +136,17 @@
                 for copy in fetch(turn + 1, part):
                     copy.start()
 
-        out[pl.ds(turn * groups, groups)] = rows[...].T.reshape(groups, 8, lanes)
+        @pl.when(turn >= 2)
+        def _():
+            send(turn - 2).wait()
+
+        stage[turn % 2] = rows[...].T.reshape(groups, 8, lanes)
+        send(turn).start()
         return carry
 
     lax.fori_loop(0, turns, body, 0)
+    for turn in range(max(turns - 2, 0), turns):
+        send(turn).wait()
 
 
 def pack(slots_row, node_arrays, owners, first, blocks):
@@ -129,14 +156,18 @@
     return pl.pallas_call(
         partial(pack_kernel, first, blocks, per_owner),
         out_shape=jax.ShapeDtypeStruct((owners * blocks, 8, lanes), F32),
-        in_specs=[in_hbm] + [in_vmem] * 4,
-        out_specs=in_vmem,
+        in_specs=[in_hbm] * 5,
+        out_specs=in_hbm,
         scratch_shapes=[
+            *[pltpu.VMEM(array.shape, F32) for array in node_arrays],
+            pltpu.VMEM((2, groups, 8, lanes), F32),
             pltpu.VMEM((count + 8, lanes), F32),
             pltpu.VMEM((lanes, lanes), F32),
             pltpu.VMEM((count // groups, 3 * lanes), BF16),
             *[pltpu.SMEM((part_slots,), jnp.int32)] * index_parts,
             pltpu.SemaphoreType.DMA((index_parts, part_slots // math.gcd(blocks * lanes, part_slots))),
+            pltpu.SemaphoreType.DMA((count // span // table_unroll, 4)),
+            pltpu.SemaphoreType.DMA((2,)),
         ],
         compiler_params=pltpu.CompilerParams(vmem_limit_bytes=vmem_limit),
     )(slots_row, *node_arrays)
@@ -299,7 +330,7 @@
 
     own_count = lax.fori_loop(0, own_blocks, leave(first_own, second_own), own_count)
     far_count = lax.fori_loop(own_blocks, blocks, leave(first_far, second_far), far_count)
-    for k in range(pairs_per_turn):
+    for k in range(2 * pairs_per_turn):
         first_own[own_count + k] = -1
         second_own[own_count + k] = -1
         first_far[far_count + k] = -1
@@ -309,7 +340,7 @@
 
 
 def tile_pairs(tile_count, tile_list, own_blocks, blocks):
-    room = tile_list.shape[1] // 2 + blocks + pairs_per_turn
+    room = tile_list.shape[1] // 2 + blocks + 2 * pairs_per_turn
     room = (room + lanes - 1) // lanes * lanes
     listed = jax.ShapeDtypeStruct((room,), jnp.int32)
     return pl.pallas_call(
@@ -324,7 +355,7 @@
 def contact_kernel(
     first_block, plan, part_refs, total_ref, firsts, seconds, list_ref,
     half_a, half_b, mask_hbm, before, out, features, seg_side, normals, masked, nodes,
-    mask, half_sems,
+    mask, hidden_ref, half_sems,
 ):
     copies = load_halves((half_a, half_b), nodes, half_sems)
     copies.append(pltpu.make_async_copy(mask_hbm, mask, half_sems.at[2]))
@@ -383,20 +414,24 @@
         p, q, r = three_parts(jnp.concatenate([state, extra], axis=0))
         return jnp.concatenate([p, p, p, q, q, r], axis=0)
 
-    def turn(index, carry):
-        pairs = []
+    def hide(index):
         for k in range(pairs_per_turn):
-            tiles = []
             for side, listed in enumerate((firsts, seconds)):
                 t = listed[index * pairs_per_turn + k]
                 live = jnp.where(t >= 0, 1.0, 0.0)
-                t = jnp.maximum(t, 0)
                 at = 96 + 2 * k + side
-                masked[at : at + 1, :] = 1.0 - mask[pl.ds(t, 1), :].astype(F32) * live
-                tiles.append(t)
+                chosen = mask[pl.ds(jnp.maximum(t, 0), 1), :].astype(F32)
+                masked[at : at + 1, :] = 1.0 - chosen * live
+        turned = [masked[:, :lanes].T, masked[:, lanes:].T]
+        hidden_ref[...] = jnp.concatenate(turned, axis=0).astype(BF16)
+
+    def turn(index, carry):
+        hidden = hidden_ref[...]
+        pairs = []
+        for k in range(pairs_per_turn):
+            tiles = [jnp.maximum(ref[index * pairs_per_turn + k], 0) for ref in (firsts, seconds)]
             block = jnp.clip(list_ref[1, tiles[0]] - first_block, 0, features.shape[0] - 1)
             pairs.append((list_ref[0, tiles[0]], list_ref[0, tiles[1]], block))
-        hidden = jnp.concatenate([masked[:, :lanes].T, masked[:, lanes:].T], axis=0).astype(BF16)
         forces = []
         for k, (one, two, block) in enumerate(pairs):
             both = jnp.concatenate([node_side(one), node_side(two)], axis=1)
@@ -436,9 +471,11 @@
             for side, block in enumerate((one, two)):
                 for i in range(3):
                     out[block // per_owner, i, pl.ds(block % per_owner, 1), :] += forces[k][side][i]
+        hide(index + 1)
         return carry
 
     turns = (total_ref[0] + pairs_per_turn - 1) // pairs_per_turn
+    hide(0)
     lax.fori_loop(0, turns, turn, 0)
 
 
@@ -474,6 +511,7 @@
             pltpu.VMEM((lanes, seg_width), F32),
             pltpu.VMEM((owners, per_owner, 8, lanes), F32),
             pltpu.VMEM(pair_mask.shape, jnp.int32),
+            pltpu.VMEM((seg_width, lanes), BF16),
             pltpu.SemaphoreType.DMA((4,)),
         ],
         compiler_params=pltpu.CompilerParams(vmem_limit_bytes=vmem_limit),
@@ -487,7 +525,7 @@
     return before, cells, after
 
 
-def sort_kernel(keys, values, out, key_s, *value_s):
+def sort_kernel(keys, values, out, stage, key_s, *value_s):
     high, low = key_s.shape[:2]
     low_bits, high_bits = low.bit_length() - 1, high.bit_length() - 1
     vector_bits = low_bits + high_bits
@@ -582,14 +620,23 @@
         lax.fori_loop(0, high // runs, lambda h, c, k=k: near(h, c, k), 0)
     vectors = high * low
     per_lane = vectors * 8 // lanes
-    used = out.shape[1] // per_lane
-    for f, ref in enumerate(value_s):
-        flat = ref.reshape(vectors * 8, lanes)
-        rows_each = lanes // vectors
-        for q in range(per_lane):
-            parts = [flat[pl.ds(q * rows_each + s, vectors, stride=8), :] for s in range(rows_each)]
-            turned = jnp.concatenate(parts, axis=0).T
-            out[f, pl.ds(q, used, stride=per_lane), :] = turned[:used]
+    used = out.shape[1] // lanes // per_lane
+    each = lanes // vectors
+    for q in range(per_lane):
+        for f, ref in enumerate(value_s):
+            flat = ref.reshape(vectors * 8, lanes)
+            rows = [flat[pl.ds(q * each + s, vectors, stride=8), :] for s in range(each)]
+            stage[f * lanes : (f + 1) * lanes, :] = jnp.concatenate(rows, axis=0).T
+
+        def place(step, carry):
+            for i in range(drain):
+                row = step * drain + i
+                at = pl.ds(pl.multiple_of((row * per_lane + q) * lanes, lanes), lanes)
+                out[:, at] = stage[pl.ds(row, 3, stride=lanes), :]
+            return carry
+
+        drain = math.gcd(used, 8)
+        lax.fori_loop(0, used // drain, place, 0)
 
 
 def order(slots_row, forces, count):
@@ -598,10 +645,14 @@
     shape = (vectors // 8, 8, 8, lanes)
     return pl.pallas_call(
         sort_kernel,
-        out_shape=jax.ShapeDtypeStruct((3, count // lanes, lanes), F32),
+        out_shape=jax.ShapeDtypeStruct((3, count), F32),
         in_specs=[in_vmem, in_vmem],
         out_specs=in_vmem,
-        scratch_shapes=[pltpu.VMEM(shape, jnp.int32)] + [pltpu.VMEM(shape, F32)] * 3,
+        scratch_shapes=[
+            pltpu.VMEM((3 * lanes, lanes), F32),
+            pltpu.VMEM(shape, jnp.int32),
+            *[pltpu.VMEM(shape, F32)] * 3,
+        ],
         compiler_params=pltpu.CompilerParams(vmem_limit_bytes=vmem_limit),
     )(slots_row.reshape(rows, lanes), forces)
 
@@ -653,7 +704,7 @@
     returned = lax.all_to_all(slot_force, both, split_axis=0, concat_axis=0)
     if per_owner % 8:
         returned = jnp.transpose(returned, (1, 0, 2, 3)).reshape(1, 3, -1, lanes)
-    return order(slots_row, returned, positions.shape[1]).reshape(3, -1)
+    return order(slots_row, returned, positions.shape[1])
 
 
 def solution(mesh):

time: 261 us -> 254 us (0.973)
  blocking collectives: 74.4 us -> 69.9 us
    all_to_all x1, blocking collectives: 74.4 us -> 69.9 us  [on_device(): returned = lax.all_to_all(slot_force, both, split_axis=0, concat_axis=0)]
where the time goes in v5:
time: 254 us; the launch traced here: 252 us
  Pallas kernels  135 us (53%)
  blocking collectives  69.9 us (28%)
  starting transfers between devices  23.3 us (9%)
  waiting for transfers between devices  16.7 us (7%)
  local copies, waits for them, and re-layouts  4.56 us (2%)
    all_to_all x1, blocking collectives, on_device(): returned = lax.all_to_all(slot_force, both, split_axis=0, concat_axis=0)  69.9 us
    pallas_call x2, Pallas kernels, pack(): pl.pallas_call(partial(pack_kernel, first, blocks, per_owner), out_shape=...  62 us
    pallas_call x2, Pallas kernels, contact_pass(): pl.pallas_call(kernel, out_shape=jax.ShapeDtypeStruct((owners, 3, per_own...  27.8 us
    pallas_call x1, Pallas kernels, order(): pl.pallas_call(sort_kernel, out_shape=jax.ShapeDtypeStruct((3, count), F3...  22.3 us
    pallas_call x2, Pallas kernels, segment_features(): pl.pallas_call(feature_kernel, out_shape=jax.ShapeDtypeStruct((quads // s...  16.8 us
    all_to_all x2, waiting for transfers between devices, on_device(): lax.all_to_all(outgoing.reshape(owners, -1, 8, lanes), both, split_axis=0...  16.7 us
    all_to_all x2, starting transfers between devices, on_device(): lax.all_to_all(outgoing.reshape(owners, -1, 8, lanes), both, split_axis=0...  13.1 us
    ppermute x2, starting transfers between devices, with_neighbours(): before = lax.ppermute(cells, axis, [(i, i + 1) for i in range(ends)])  7.58 us
  transfers between devices with their start and end apart: 6, of which 1 were waited for; matrix products, arithmetic and copies ran while one was open for 1% of the time, Pallas kernels for 23%

profile of v5, /device:TPU:0, one launch (start us, length us, event | category | flops | bytes accessed | tf_op | source)
XLA Modules:
  0.0 252.4 jit_solution(5592334273342392358)
XLA Ops:
  0.0 31.0 %shard_map.93 = f32[256,8,128]{2,1,0:T(8,128)} custom-call(s32[65536]{0:T(1024)} %bitcast.58, f32[3,49152]{1,0:T(4,128)} %place_hbm.3, f32[3,49152]{1,0:T(4,128)} %speed_hbm.3, f32[1,49152]{1,0:T(1,128)} %bitcast.61, f32[1,49152]{1,0:T(1,128)} %bitcast.63), custom_call_target="tpu_custom_call" | custom-call | tf_op jit(solution)/shard_map/pallas_call | solution.py:156
  31.0 7.3 %all-to-all-start.1 = ((f32[32,8,8,128]{3,2,1,0:T(8,128)}), f32[32,8,8,128]{3,2,1,0:T(8,128)S(1)}, u32[]{:S(2)}, u32[]{:S(2)}) async-start(f32[32,8,8,128]{3,2,1,0:T(8,128)} %bitcast.57), calls=%async_computation.1 | async-start | bytes 2097152 | tf_op jit(solution)/shard_map/all_to_all | solution.py:681
  38.3 31.0 %shard_map.91 = f32[256,8,128]{2,1,0:T(8,128)} custom-call(s32[65536]{0:T(1024)} %bitcast.59, f32[3,49152]{1,0:T(4,128)} %place_hbm.3, f32[3,49152]{1,0:T(4,128)} %speed_hbm.3, f32[1,49152]{1,0:T(1,128)} %bitcast.62, f32[1,49152]{1,0:T(1,128)} %bitcast.64), custom_call_target="tpu_custom_call" | custom-call | tf_op jit(solution)/shard_map/pallas_call | solution.py:156
  69.3 0.0 all-to-all-done.1.half_b.refs_7_.refs_8_
  69.3 1.0 copy-done
  70.3 5.8 %all-to-all-start = ((f32[32,8,8,128]{3,2,1,0:T(8,128)}), f32[32,8,8,128]{3,2,1,0:T(8,128)S(1)}, u32[]{:S(2)}, u32[]{:S(2)}) async-start(f32[32,8,8,128]{3,2,1,0:T(8,128)} %bitcast.56), calls=%async_computation | async-start | bytes 2097152 | tf_op jit(solution)/shard_map/all_to_all | solution.py:681
  76.8 0.0 slice-start
  76.8 0.7 slice-done
  77.6 6.2 %shard_map.92 = (s32[2]{0:T(128)}, s32[640]{0:T(1024)}, s32[640]{0:T(1024)}, s32[640]{0:T(1024)}, s32[640]{0:T(1024)}) custom-call(s32[1]{0:T(128)S(6)} %copy.23.count_ref, s32[2,1024]{1,0:T(2,128)} %refs_6_.1), custom_call_target="tpu_custom_call" | custom-call | tf_op jit(solution)/shard_map/pallas_call | solution.py:346
  83.8 0.6 fusion.7
  84.4 0.6 add_select_fusion.2.place
  85.0 0.6 add_select_fusion.place
  85.7 16.7 %all-to-all-done.half_a.refs_6_.refs_7_ = f32[32,8,8,128]{3,2,1,0:T(8,128)S(1)} async-done(((f32[32,8,8,128]{3,2,1,0:T(8,128)}), f32[32,8,8,128]{3,2,1,0:T(8,128)S(1)}, u32[]{:S(2)}, u32[]{:S(2)}) %all-to-all-start) | async-done | bytes 1048608 | tf_op jit(solution)/shard_map/all_to_all | solution.py:681
  102.4 1.0 copy-done.1
  103.4 5.6 %shard_map.94.refs_0_ = f32[2,16,256]{2,1,0:T(8,128)} custom-call(s32[2048]{0:T(1024)} %bitcast.67, f32[32,8,8,128]{3,2,1,0:T(8,128)} %copy-done.1, f32[32,8,8,128]{3,2,1,0:T(8,128)} %copy-done, s32[4,4,128]{2,1,0:T(4,128)} %add_select_fusion.2.place), custom_call_target="tpu_custom_call" | custom-call | tf_op jit(solution)/shard_map/pallas_call | solution.py:257
  109.0 1.3 collective-permute-start.1
  110.3 4.5 %collective-permute-start = (f32[2,16,256]{2,1,0:T(8,128)}, f32[2,16,256]{2,1,0:T(8,128)S(1)}, u32[]{:S(2)}, u32[]{:S(2)}) collective-permute-start(f32[2,16,256]{2,1,0:T(8,128)} %shard_map.94.refs_0_), channel_id=1, source_target_pairs={{0,4},{4,8},{8,12},{12,16},{16,20},{20,24},{24,28},{1,5},{5,9},{9,... | collective-permute-start | bytes 98312 | tf_op jit(solution)/shard_map/ppermute | solution.py:523
  114.9 0.6 copy.16
  115.5 11.2 %shard_map.95.refs_1_ = f32[6,16,256]{2,1,0:T(8,128)} custom-call(s32[6144]{0:T(1024)} %bitcast.66, f32[32,8,8,128]{3,2,1,0:T(8,128)} %copy-done.1, f32[32,8,8,128]{3,2,1,0:T(8,128)} %copy-done, s32[4,12,128]{2,1,0:T(8,128)} %add_select_fusion.place), custom_call_target="tpu_custom_call" | custom-call | tf_op jit(solution)/shard_map/pallas_call | solution.py:257
  126.7 0.0 collective-permute-done.1
  126.7 0.0 collective-permute-done
  126.8 1.3 collective-permute-start.3
  128.1 3.0 %collective-permute-start.2 = (f32[3,2,16,256]{3,2,1,0:T(8,128)S(1)}, f32[3,2,16,256]{3,2,1,0:T(8,128)S(1)}, u32[]{:S(2)}, u32[]{:S(2)}) collective-permute-start(f32[3,2,16,256]{3,2,1,0:T(8,128)S(1)} %pad_maximum_fusion.refs_1_), channel_id=1, source_target_pairs={{0,1},{1,2},{2,3},{4,5},{5,6},{6,7},{8,9},{9,10},{10,11},{12,13},{... | collective-permute-start | bytes 294920 | tf_op jit(solution)/shard_map/ppermute | solution.py:523
  131.1 0.6 fusion.11
  131.7 10.7 %shard_map.96.refs_10_ = f32[32,3,16,128]{3,2,1,0:T(8,128)} custom-call(f32[2,16,256]{2,1,0:T(8,128)} %shard_map.94.refs_0_, f32[6,16,256]{2,1,0:T(8,128)} %shard_map.95.refs_1_, s32[1]{0:T(128)} %get-tuple-element.19.refs_2_, s32[640]{0:T(1024)} %get-tuple-element.17.refs_3_, s32[640]{0:T(1024)} %get-tuple-element.18.refs_4_, s32[2,1024]{1,0:T(2,128)} %refs_6_.1, ...), custom_call_target="tpu_custom_call" | custom-call | tf_op jit(solution)/shard_map/pallas_call | solution.py:502
  142.4 0.0 collective-permute-done.3.refs_2_
  142.4 0.0 collective-permute-done.2.refs_0_
  142.5 0.6 copy-done.5
  143.1 0.0 copy-done.6
  143.1 17.1 %shard_map.97 = f32[32,3,16,128]{3,2,1,0:T(8,128)} custom-call(f32[3,2,16,256]{3,2,1,0:T(8,128)} %copy-done.6, f32[3,2,16,256]{3,2,1,0:T(8,128)} %copy-done.2, f32[3,2,16,256]{3,2,1,0:T(8,128)} %copy-done.5, s32[1]{0:T(128)} %get-tuple-element.20.refs_3_, s32[640]{0:T(1024)} %get-tuple-element.15.refs_4_, s32[640]{0:T(1024)} %get-tuple-element.16.refs_5_, ...), custom_call_target="tpu_custom_call" | custom-call | tf_op jit(solution)/shard_map/pallas_call | solution.py:502
  160.2 69.9 %all_to_all.15.values = f32[32,3,16,128]{3,2,1,0:T(8,128)} all-to-all(f32[32,3,16,128]{3,2,1,0:T(8,128)} %shard_map.97), channel_id=1, replica_groups=mesh['wide'=8,'narrow'=4] {'wide','narrow'}, dimensions={0} | all-to-all | bytes 1572864 | tf_op jit(solution)/shard_map/all_to_all | solution.py:704
  230.2 22.3 %shard_map.98 = f32[3,49152]{1,0:T(4,128)} custom-call(s32[512,128]{1,0:T(8,128)} %bitcast.60, f32[32,3,16,128]{3,2,1,0:T(8,128)} %all_to_all.15.values), custom_call_target="tpu_custom_call" | custom-call | tf_op jit(solution)/shard_map/pallas_call | solution.py:646
  (17 shorter events, 0.1 us)
Async XLA Ops:
  31.0 38.3 %all-to-all-start.1 = ((f32[32,8,8,128]{3,2,1,0:T(8,128)}), f32[32,8,8,128]{3,2,1,0:T(8,128)S(1)}, u32[]{:S(2)}, u32[]{:S(2)}) async-start(f32[32,8,8,128]{3,2,1,0:T(8,128)} %bitcast.57), calls=%async_computation.1 | async-start | bytes 2097152 | tf_op jit(solution)/shard_map/all_to_all | solution.py:681
  69.3 1.0 copy-start
  70.3 32.1 %all-to-all-start = ((f32[32,8,8,128]{3,2,1,0:T(8,128)}), f32[32,8,8,128]{3,2,1,0:T(8,128)S(1)}, u32[]{:S(2)}, u32[]{:S(2)}) async-start(f32[32,8,8,128]{3,2,1,0:T(8,128)} %bitcast.56), calls=%async_computation | async-start | bytes 2097152 | tf_op jit(solution)/shard_map/all_to_all | solution.py:681
  76.8 0.7 slice-start
  77.5 6.2 %copy-start.4 = (s32[2048,4]{0,1:T(4,128)S(1)}, s32[2048,4]{0,1:T(4,128)}, u32[]{:S(2)}) copy-start(s32[2048,4]{0,1:T(4,128)} %param.14) | copy-start | bytes 98308
  102.4 1.0 copy-start.1
  109.0 17.7 %collective-permute-start.1 = (f32[2,16,256]{2,1,0:T(8,128)}, f32[2,16,256]{2,1,0:T(8,128)S(1)}, u32[]{:S(2)}, u32[]{:S(2)}) collective-permute-start(f32[2,16,256]{2,1,0:T(8,128)} %shard_map.94.refs_0_), channel_id=1, source_target_pairs={{4,0},{8,4},{12,8},{16,12},{20,16},{24,20},{28,24},{5,1},{9,5},{13... | collective-permute-start | bytes 98312 | tf_op jit(solution)/shard_map/ppermute | solution.py:524
  110.3 16.4 %collective-permute-start = (f32[2,16,256]{2,1,0:T(8,128)}, f32[2,16,256]{2,1,0:T(8,128)S(1)}, u32[]{:S(2)}, u32[]{:S(2)}) collective-permute-start(f32[2,16,256]{2,1,0:T(8,128)} %shard_map.94.refs_0_), channel_id=1, source_target_pairs={{0,4},{4,8},{8,12},{12,16},{16,20},{20,24},{24,28},{1,5},{5,9},{9,... | collective-permute-start | bytes 98312 | tf_op jit(solution)/shard_map/ppermute | solution.py:523
  115.5 11.2 %copy-start.3 = (f32[2,16,256]{2,1,0:T(8,128)S(1)}, f32[2,16,256]{2,1,0:T(8,128)}, u32[]{:S(2)}) copy-start(f32[2,16,256]{2,1,0:T(8,128)} %shard_map.94.refs_0_) | copy-start | bytes 98308
  126.7 4.4 %copy-start.7 = (s32[2]{0:T(128)S(1)}, s32[2]{0:T(128)}, u32[]{:S(2)}) copy-start(s32[2]{0:T(128)} %get-tuple-element.14) | copy-start | bytes 28
  126.7 15.7 %copy-start.2 = (f32[3,2,16,256]{3,2,1,0:T(8,128)}, f32[3,2,16,256]{3,2,1,0:T(8,128)S(1)}, u32[]{:S(2)}) copy-start(f32[3,2,16,256]{3,2,1,0:T(8,128)S(1)} %pad_maximum_fusion.refs_1_) | copy-start | bytes 294916
  126.8 15.7 %collective-permute-start.3 = (f32[3,2,16,256]{3,2,1,0:T(8,128)S(1)}, f32[3,2,16,256]{3,2,1,0:T(8,128)S(1)}, u32[]{:S(2)}, u32[]{:S(2)}) collective-permute-start(f32[3,2,16,256]{3,2,1,0:T(8,128)S(1)} %pad_maximum_fusion.refs_1_), channel_id=1, source_target_pairs={{1,0},{2,1},{3,2},{5,4},{6,5},{7,6},{9,8},{10,9},{11,10},{13,12},{... | collective-permute-start | bytes 294920 | tf_op jit(solution)/shard_map/ppermute | solution.py:524
  128.1 14.4 %collective-permute-start.2 = (f32[3,2,16,256]{3,2,1,0:T(8,128)S(1)}, f32[3,2,16,256]{3,2,1,0:T(8,128)S(1)}, u32[]{:S(2)}, u32[]{:S(2)}) collective-permute-start(f32[3,2,16,256]{3,2,1,0:T(8,128)S(1)} %pad_maximum_fusion.refs_1_), channel_id=1, source_target_pairs={{0,1},{1,2},{2,3},{4,5},{5,6},{6,7},{8,9},{9,10},{10,11},{12,13},{... | collective-permute-start | bytes 294920 | tf_op jit(solution)/shard_map/ppermute | solution.py:523
  142.4 0.6 copy-start.5
  142.4 0.7 copy-start.6

commit v6 on v5

--- a/solution.py
+++ b/solution.py
@@ -534,7 +534,7 @@
     lane = lax.broadcasted_iota(jnp.int32, (8, lanes), 1)
     sub = lax.broadcasted_iota(jnp.int32, (8, lanes), 0)
     inside = (lane * 8 + sub) << vector_bits
-    runs = math.gcd(high, 2)
+    runs = math.gcd(high, 4)
     wide = (runs * low, 8, lanes)
     lane_w = lax.broadcasted_iota(jnp.int32, wide, 2)
     sub_w = lax.broadcasted_iota(jnp.int32, wide, 1)

time: 254 us -> 254 us (level)
  Pallas kernels: 135 us -> 155 us
  blocking collectives: 69.9 us -> 54.9 us
  waiting for transfers between devices: 16.7 us -> 12.5 us
    pallas_call x2, Pallas kernels: 27.8 us -> 44 us  [contact_pass(): pl.pallas_call(kernel, out_shape=jax.ShapeDtypeStruct((owners, 3, per_own...]
    all_to_all x1, blocking collectives: 69.9 us -> 54.9 us  [on_device(): returned = lax.all_to_all(slot_force, both, split_axis=0, concat_axis=0)]
    pallas_call x1, Pallas kernels: 6.22 us -> 10.5 us  [tile_pairs(): pl.pallas_call(partial(pair_kernel, own_blocks), out_shape=[jax.ShapeDtyp...]
    all_to_all x2, waiting for transfers between devices: 16.7 us -> 12.5 us  [on_device(): lax.all_to_all(outgoing.reshape(owners, -1, 8, lanes), both, split_axis=0...]
  transfers between devices with their start and end apart: 6 -> 6, of which waited for: 1 -> 1; matrix products, arithmetic and copies ran while one was open for 1% -> 1% of each run, Pallas kernels for 23% -> 27%
where the time goes in v6:
time: 254 us; the launch traced here: 253 us
  Pallas kernels  155 us (61%)
  blocking collectives  54.9 us (22%)
  starting transfers between devices  23.3 us (9%)
  waiting for transfers between devices  12.5 us (5%)
  local copies, waits for them, and re-layouts  4.56 us (2%)
    pallas_call x2, Pallas kernels, pack(): pl.pallas_call(partial(pack_kernel, first, blocks, per_owner), out_shape=...  62 us
    all_to_all x1, blocking collectives, on_device(): returned = lax.all_to_all(slot_force, both, split_axis=0, concat_axis=0)  54.9 us
    pallas_call x2, Pallas kernels, contact_pass(): pl.pallas_call(kernel, out_shape=jax.ShapeDtypeStruct((owners, 3, per_own...  44 us
    pallas_call x1, Pallas kernels, order(): pl.pallas_call(sort_kernel, out_shape=jax.ShapeDtypeStruct((3, count), F3...  21.6 us
    pallas_call x2, Pallas kernels, segment_features(): pl.pallas_call(feature_kernel, out_shape=jax.ShapeDtypeStruct((quads // s...  16.8 us
    all_to_all x2, starting transfers between devices, on_device(): lax.all_to_all(outgoing.reshape(owners, -1, 8, lanes), both, split_axis=0...  13.1 us
    all_to_all x2, waiting for transfers between devices, on_device(): lax.all_to_all(outgoing.reshape(owners, -1, 8, lanes), both, split_axis=0...  12.5 us
    pallas_call x1, Pallas kernels, tile_pairs(): pl.pallas_call(partial(pair_kernel, own_blocks), out_shape=[jax.ShapeDtyp...  10.5 us
  transfers between devices with their start and end apart: 6, of which 1 were waited for; matrix products, arithmetic and copies ran while one was open for 1% of the time, Pallas kernels for 27%

profile of v6, /device:TPU:0, one launch (start us, length us, event | category | flops | bytes accessed | tf_op | source)
XLA Modules:
  0.0 253.0 jit_solution(8729139421982104265)
XLA Ops:
  0.0 31.0 %shard_map.93 = f32[256,8,128]{2,1,0:T(8,128)} custom-call(s32[65536]{0:T(1024)} %bitcast.58, f32[3,49152]{1,0:T(4,128)} %place_hbm.3, f32[3,49152]{1,0:T(4,128)} %speed_hbm.3, f32[1,49152]{1,0:T(1,128)} %bitcast.61, f32[1,49152]{1,0:T(1,128)} %bitcast.63), custom_call_target="tpu_custom_call" | custom-call | tf_op jit(solution)/shard_map/pallas_call | solution.py:156
  31.0 7.3 %all-to-all-start.1 = ((f32[32,8,8,128]{3,2,1,0:T(8,128)}), f32[32,8,8,128]{3,2,1,0:T(8,128)S(1)}, u32[]{:S(2)}, u32[]{:S(2)}) async-start(f32[32,8,8,128]{3,2,1,0:T(8,128)} %bitcast.57), calls=%async_computation.1 | async-start | bytes 2097152 | tf_op jit(solution)/shard_map/all_to_all | solution.py:681
  38.3 31.0 %shard_map.91 = f32[256,8,128]{2,1,0:T(8,128)} custom-call(s32[65536]{0:T(1024)} %bitcast.59, f32[3,49152]{1,0:T(4,128)} %place_hbm.3, f32[3,49152]{1,0:T(4,128)} %speed_hbm.3, f32[1,49152]{1,0:T(1,128)} %bitcast.62, f32[1,49152]{1,0:T(1,128)} %bitcast.64), custom_call_target="tpu_custom_call" | custom-call | tf_op jit(solution)/shard_map/pallas_call | solution.py:156
  69.3 0.0 all-to-all-done.1.half_b.refs_7_.refs_8_
  69.3 1.0 copy-done
  70.3 5.8 %all-to-all-start = ((f32[32,8,8,128]{3,2,1,0:T(8,128)}), f32[32,8,8,128]{3,2,1,0:T(8,128)S(1)}, u32[]{:S(2)}, u32[]{:S(2)}) async-start(f32[32,8,8,128]{3,2,1,0:T(8,128)} %bitcast.56), calls=%async_computation | async-start | bytes 2097152 | tf_op jit(solution)/shard_map/all_to_all | solution.py:681
  76.8 0.0 slice-start
  76.8 0.7 slice-done
  77.6 10.5 %shard_map.92 = (s32[2]{0:T(128)}, s32[640]{0:T(1024)}, s32[640]{0:T(1024)}, s32[640]{0:T(1024)}, s32[640]{0:T(1024)}) custom-call(s32[1]{0:T(128)S(6)} %copy.23.count_ref, s32[2,1024]{1,0:T(2,128)} %refs_6_.1), custom_call_target="tpu_custom_call" | custom-call | tf_op jit(solution)/shard_map/pallas_call | solution.py:346
  88.1 0.6 fusion.7
  88.7 0.6 add_select_fusion.2.place
  89.3 0.6 add_select_fusion.place
  89.9 12.5 %all-to-all-done.half_a.refs_6_.refs_7_ = f32[32,8,8,128]{3,2,1,0:T(8,128)S(1)} async-done(((f32[32,8,8,128]{3,2,1,0:T(8,128)}), f32[32,8,8,128]{3,2,1,0:T(8,128)S(1)}, u32[]{:S(2)}, u32[]{:S(2)}) %all-to-all-start) | async-done | bytes 1048608 | tf_op jit(solution)/shard_map/all_to_all | solution.py:681
  102.4 1.0 copy-done.1
  103.4 5.6 %shard_map.94.refs_0_ = f32[2,16,256]{2,1,0:T(8,128)} custom-call(s32[2048]{0:T(1024)} %bitcast.67, f32[32,8,8,128]{3,2,1,0:T(8,128)} %copy-done.1, f32[32,8,8,128]{3,2,1,0:T(8,128)} %copy-done, s32[4,4,128]{2,1,0:T(4,128)} %add_select_fusion.2.place), custom_call_target="tpu_custom_call" | custom-call | tf_op jit(solution)/shard_map/pallas_call | solution.py:257
  109.0 1.3 collective-permute-start.1
  110.3 4.5 %collective-permute-start = (f32[2,16,256]{2,1,0:T(8,128)}, f32[2,16,256]{2,1,0:T(8,128)S(1)}, u32[]{:S(2)}, u32[]{:S(2)}) collective-permute-start(f32[2,16,256]{2,1,0:T(8,128)} %shard_map.94.refs_0_), channel_id=1, source_target_pairs={{0,4},{4,8},{8,12},{12,16},{16,20},{20,24},{24,28},{1,5},{5,9},{9,... | collective-permute-start | bytes 98312 | tf_op jit(solution)/shard_map/ppermute | solution.py:523
  114.9 0.6 copy.16
  115.5 11.2 %shard_map.95.refs_1_ = f32[6,16,256]{2,1,0:T(8,128)} custom-call(s32[6144]{0:T(1024)} %bitcast.66, f32[32,8,8,128]{3,2,1,0:T(8,128)} %copy-done.1, f32[32,8,8,128]{3,2,1,0:T(8,128)} %copy-done, s32[4,12,128]{2,1,0:T(8,128)} %add_select_fusion.place), custom_call_target="tpu_custom_call" | custom-call | tf_op jit(solution)/shard_map/pallas_call | solution.py:257
  126.7 0.0 collective-permute-done.1
  126.7 0.0 collective-permute-done
  126.7 1.3 collective-permute-start.3
  128.0 3.0 %collective-permute-start.2 = (f32[3,2,16,256]{3,2,1,0:T(8,128)S(1)}, f32[3,2,16,256]{3,2,1,0:T(8,128)S(1)}, u32[]{:S(2)}, u32[]{:S(2)}) collective-permute-start(f32[3,2,16,256]{3,2,1,0:T(8,128)S(1)} %pad_maximum_fusion.refs_1_), channel_id=1, source_target_pairs={{0,1},{1,2},{2,3},{4,5},{5,6},{6,7},{8,9},{9,10},{10,11},{12,13},{... | collective-permute-start | bytes 294920 | tf_op jit(solution)/shard_map/ppermute | solution.py:523
  131.1 0.6 fusion.11
  131.7 14.7 %shard_map.96.refs_10_ = f32[32,3,16,128]{3,2,1,0:T(8,128)} custom-call(f32[2,16,256]{2,1,0:T(8,128)} %shard_map.94.refs_0_, f32[6,16,256]{2,1,0:T(8,128)} %shard_map.95.refs_1_, s32[1]{0:T(128)} %get-tuple-element.19.refs_2_, s32[640]{0:T(1024)} %get-tuple-element.17.refs_3_, s32[640]{0:T(1024)} %get-tuple-element.18.refs_4_, s32[2,1024]{1,0:T(2,128)} %refs_6_.1, ...), custom_call_target="tpu_custom_call" | custom-call | tf_op jit(solution)/shard_map/pallas_call | solution.py:502
  146.4 0.0 collective-permute-done.3.refs_2_
  146.5 0.0 collective-permute-done.2.refs_0_
  146.5 0.6 copy-done.5
  147.1 0.0 copy-done.6
  147.1 29.3 %shard_map.97 = f32[32,3,16,128]{3,2,1,0:T(8,128)} custom-call(f32[3,2,16,256]{3,2,1,0:T(8,128)} %copy-done.6, f32[3,2,16,256]{3,2,1,0:T(8,128)} %copy-done.2, f32[3,2,16,256]{3,2,1,0:T(8,128)} %copy-done.5, s32[1]{0:T(128)} %get-tuple-element.20.refs_3_, s32[640]{0:T(1024)} %get-tuple-element.15.refs_4_, s32[640]{0:T(1024)} %get-tuple-element.16.refs_5_, ...), custom_call_target="tpu_custom_call" | custom-call | tf_op jit(solution)/shard_map/pallas_call | solution.py:502
  176.4 54.9 %all_to_all.15.values = f32[32,3,16,128]{3,2,1,0:T(8,128)} all-to-all(f32[32,3,16,128]{3,2,1,0:T(8,128)} %shard_map.97), channel_id=1, replica_groups=mesh['wide'=8,'narrow'=4] {'wide','narrow'}, dimensions={0} | all-to-all | bytes 1572864 | tf_op jit(solution)/shard_map/all_to_all | solution.py:704
  231.3 21.6 %shard_map.98 = f32[3,49152]{1,0:T(4,128)} custom-call(s32[512,128]{1,0:T(8,128)} %bitcast.60, f32[32,3,16,128]{3,2,1,0:T(8,128)} %all_to_all.15.values), custom_call_target="tpu_custom_call" | custom-call | tf_op jit(solution)/shard_map/pallas_call | solution.py:646
  (17 shorter events, 0.1 us)
Async XLA Ops:
  31.0 38.3 %all-to-all-start.1 = ((f32[32,8,8,128]{3,2,1,0:T(8,128)}), f32[32,8,8,128]{3,2,1,0:T(8,128)S(1)}, u32[]{:S(2)}, u32[]{:S(2)}) async-start(f32[32,8,8,128]{3,2,1,0:T(8,128)} %bitcast.57), calls=%async_computation.1 | async-start | bytes 2097152 | tf_op jit(solution)/shard_map/all_to_all | solution.py:681
  69.3 1.0 copy-start
  70.3 32.1 %all-to-all-start = ((f32[32,8,8,128]{3,2,1,0:T(8,128)}), f32[32,8,8,128]{3,2,1,0:T(8,128)S(1)}, u32[]{:S(2)}, u32[]{:S(2)}) async-start(f32[32,8,8,128]{3,2,1,0:T(8,128)} %bitcast.56), calls=%async_computation | async-start | bytes 2097152 | tf_op jit(solution)/shard_map/all_to_all | solution.py:681
  76.8 0.7 slice-start
  77.5 10.5 %copy-start.4 = (s32[2048,4]{0,1:T(4,128)S(1)}, s32[2048,4]{0,1:T(4,128)}, u32[]{:S(2)}) copy-start(s32[2048,4]{0,1:T(4,128)} %param.14) | copy-start | bytes 98308
  102.4 1.0 copy-start.1
  109.0 17.7 %collective-permute-start.1 = (f32[2,16,256]{2,1,0:T(8,128)}, f32[2,16,256]{2,1,0:T(8,128)S(1)}, u32[]{:S(2)}, u32[]{:S(2)}) collective-permute-start(f32[2,16,256]{2,1,0:T(8,128)} %shard_map.94.refs_0_), channel_id=1, source_target_pairs={{4,0},{8,4},{12,8},{16,12},{20,16},{24,20},{28,24},{5,1},{9,5},{13... | collective-permute-start | bytes 98312 | tf_op jit(solution)/shard_map/ppermute | solution.py:524
  110.3 16.4 %collective-permute-start = (f32[2,16,256]{2,1,0:T(8,128)}, f32[2,16,256]{2,1,0:T(8,128)S(1)}, u32[]{:S(2)}, u32[]{:S(2)}) collective-permute-start(f32[2,16,256]{2,1,0:T(8,128)} %shard_map.94.refs_0_), channel_id=1, source_target_pairs={{0,4},{4,8},{8,12},{12,16},{16,20},{20,24},{24,28},{1,5},{5,9},{9,... | collective-permute-start | bytes 98312 | tf_op jit(solution)/shard_map/ppermute | solution.py:523
  115.5 11.2 %copy-start.3 = (f32[2,16,256]{2,1,0:T(8,128)S(1)}, f32[2,16,256]{2,1,0:T(8,128)}, u32[]{:S(2)}) copy-start(f32[2,16,256]{2,1,0:T(8,128)} %shard_map.94.refs_0_) | copy-start | bytes 98308
  126.7 4.4 %copy-start.7 = (s32[2]{0:T(128)S(1)}, s32[2]{0:T(128)}, u32[]{:S(2)}) copy-start(s32[2]{0:T(128)} %get-tuple-element.14) | copy-start | bytes 28
  126.7 19.7 %copy-start.2 = (f32[3,2,16,256]{3,2,1,0:T(8,128)}, f32[3,2,16,256]{3,2,1,0:T(8,128)S(1)}, u32[]{:S(2)}) copy-start(f32[3,2,16,256]{3,2,1,0:T(8,128)S(1)} %pad_maximum_fusion.refs_1_) | copy-start | bytes 294916
  126.7 19.7 %collective-permute-start.3 = (f32[3,2,16,256]{3,2,1,0:T(8,128)S(1)}, f32[3,2,16,256]{3,2,1,0:T(8,128)S(1)}, u32[]{:S(2)}, u32[]{:S(2)}) collective-permute-start(f32[3,2,16,256]{3,2,1,0:T(8,128)S(1)} %pad_maximum_fusion.refs_1_), channel_id=1, source_target_pairs={{1,0},{2,1},{3,2},{5,4},{6,5},{7,6},{9,8},{10,9},{11,10},{13,12},{... | collective-permute-start | bytes 294920 | tf_op jit(solution)/shard_map/ppermute | solution.py:524
  128.0 18.4 %collective-permute-start.2 = (f32[3,2,16,256]{3,2,1,0:T(8,128)S(1)}, f32[3,2,16,256]{3,2,1,0:T(8,128)S(1)}, u32[]{:S(2)}, u32[]{:S(2)}) collective-permute-start(f32[3,2,16,256]{3,2,1,0:T(8,128)S(1)} %pad_maximum_fusion.refs_1_), channel_id=1, source_target_pairs={{0,1},{1,2},{2,3},{4,5},{5,6},{6,7},{8,9},{9,10},{10,11},{12,13},{... | collective-permute-start | bytes 294920 | tf_op jit(solution)/shard_map/ppermute | solution.py:523
  146.5 0.6 copy-start.5
  146.5 0.7 copy-start.6
